TPU v7x, 256 devices: a whole 4x4x8 slice. The times are simulated.
256 devices in a mesh: row: 16 (over z, core), col: 16 (over y, x).
Axes of the slice: x: 4, y: 4, z: 8, core: 2. Of those that a mesh axis runs over, the one named last changes fastest.
Arguments:
- node_input: bfloat16 [32768, 128], P(('row', 'col')), may hold values from -6 to 6
- adj_tiles: bfloat16 [16, 16, 128, 128, 128], P('row', 'col'), may hold values from -0.046875 to 0.046875
- tile_row: int32 [16, 16, 128], P('row', 'col'), may hold values from 0 to 15
- tile_col: int32 [16, 16, 128], P('row', 'col'), may hold values from 0 to 15
- weight_in: bfloat16 [128, 512], replicated, may hold values from -0.5 to 0.5
- weight_out: bfloat16 [512, 128], replicated, may hold values from -0.25 to 0.25
- logit_grad: bfloat16 [32768, 128], P(('row', 'col')), may hold values from -6 to 6
Outputs:
- logits: float32 [32768, 128], P(('row', 'col'))
- w_in_grad: float32 [128, 512], replicated
- w_out_grad: float32 [512, 128], replicated
Inputs may be any that keep to these rules, and one draw needn't show every extreme that they name: tile_row[r, c, k] names the tile of nodes within block row r: the nodes 128 * (r * 16 + tile_row) onward; a device's tiles may repeat a position. tile_col[r, c, k] = q names the tile of nodes 128 * (q * 16 + c) onward; some columns are named far more often than others.
All inputs are finite; a program needn't handle non-finite values.
Results may differ from a plain program's by a relative error of at most 0.0045.
Values may be sent and summed in bfloat16 or wider, within the bound.
No kernel may reach another device: no remote copies, remote signals or barrier semaphores. Data moves between devices by JAX's collectives and lax.ppermute only.
A program may use at most 128 MiB of HBM per device.

v0:
```python
import math

import jax
import jax.numpy as jnp
from jax import lax
from jax.sharding import PartitionSpec as P


def spread_tiles(tile_vals, target_ids, source_ids, features, out_tiles, transpose):
    tile_size = tile_vals.shape[-1]
    feat_width = features.shape[-1]
    blocks = features.reshape(-1, tile_size, feat_width)
    tile_total = tile_vals.shape[0]
    block_size = 32
    full_float = features.dtype == jnp.float32
    pattern = "tji,tjf->tif" if transpose else "tij,tjf->tif"

    def add_block(totals, block_number):
        first_tile = block_number * block_size
        chosen = lax.dynamic_slice_in_dim(tile_vals, first_tile, block_size, 0)
        target = lax.dynamic_slice_in_dim(target_ids, first_tile, block_size, 0)
        source = lax.dynamic_slice_in_dim(source_ids, first_tile, block_size, 0)
        picked = blocks[source]
        if full_float:
            product = jnp.einsum(
                pattern, chosen.astype(jnp.float32), picked, precision=lax.Precision.HIGHEST
            )
        else:
            product = jnp.einsum(pattern, chosen, picked, preferred_element_type=jnp.float32)
        return (totals.at[target].add(product), None)

    totals = jnp.zeros((out_tiles, tile_size, feat_width), jnp.float32)
    totals, _ = lax.scan(add_block, totals, jnp.arange(tile_total // block_size, dtype=jnp.int32))
    return totals.reshape(out_tiles * tile_size, feat_width)


def on_device(node_input, adj_tiles, tile_row, tile_col, weight_in, weight_out, logit_grad):
    tile_size = adj_tiles.shape[-1]
    tile_vals = adj_tiles.reshape(-1, tile_size, tile_size)
    row_ids = tile_row.reshape(-1)
    col_ids = tile_col.reshape(-1)
    local_blocks = node_input.shape[0] // tile_size
    row_span = local_blocks * lax.axis_size("col")
    col_span = local_blocks * lax.axis_size("row")
    node_total = node_input.shape[0] * lax.axis_size("row") * lax.axis_size("col")
    scale = 1.0 / math.sqrt(node_total)
    gathered_in = lax.all_gather(node_input, "row", axis=0, tiled=True)
    partial_in = spread_tiles(tile_vals, row_ids, col_ids, gathered_in, row_span, False)
    agg_in = lax.psum_scatter(partial_in, "col", scatter_dimension=0, tiled=True).astype(
        jnp.bfloat16
    )
    pre_act = jnp.dot(agg_in, weight_in, preferred_element_type=jnp.float32)
    hidden = jax.nn.silu(pre_act).astype(jnp.bfloat16)
    out_weight = weight_out.astype(jnp.float32)
    gathered_hid = lax.all_gather(hidden, "row", axis=0, tiled=True)
    partial_hid = spread_tiles(tile_vals, row_ids, col_ids, gathered_hid, row_span, False)
    agg_hid = lax.psum_scatter(partial_hid, "col", scatter_dimension=0, tiled=True)
    logits = jnp.dot(agg_hid, out_weight, precision=lax.Precision.HIGHEST)
    grad_logit = logit_grad.astype(jnp.float32) * scale
    grad_agg = jnp.dot(logit_grad, weight_out.T, preferred_element_type=jnp.float32) * scale
    gathered_grad = lax.all_gather(grad_agg, "col", axis=0, tiled=True)
    partial_grad = spread_tiles(tile_vals, col_ids, row_ids, gathered_grad, col_span, True)
    grad_hidden = lax.psum_scatter(partial_grad, "row", scatter_dimension=0, tiled=True)
    out_term = jnp.dot(agg_hid.T, grad_logit, precision=lax.Precision.HIGHEST)
    sigmoid_vals = jax.nn.sigmoid(pre_act)
    grad_pre = grad_hidden * sigmoid_vals * (1.0 + pre_act * (1.0 - sigmoid_vals))
    in_term = jnp.dot(agg_in.astype(jnp.float32).T, grad_pre, precision=lax.Precision.HIGHEST)
    w_in_grad, w_out_grad = lax.psum((in_term, out_term), ("row", "col"))
    return (logits, w_in_grad, w_out_grad)


def solution(mesh):
    placed = (
        P(("row", "col"), None),
        P("row", "col", None, None, None),
        P("row", "col", None),
        P("row", "col", None),
        P(),
        P(),
        P(("row", "col"), None),
    )
    return jax.shard_map(
        on_device,
        mesh=mesh,
        in_specs=placed,
        out_specs=(P(("row", "col"), None), P(), P()),
        check_vma=False,
    )
```

profile of v0, /device:TPU:1, one launch (start us, length us, event | category | flops | bytes accessed | tf_op | source)
XLA Modules:
  0.0 792.9 jit_solution(13073565799659312061)
XLA Ops:
  7.2 24.4 %all_gather.9 = bf16[2048,128]{1,0:T(8,128)(2,1)} all-gather(bf16[128,128]{1,0:T(8,128)(2,1)} %param.13), channel_id=1, replica_groups=mesh['row'=16,'col'=16] {'row'}, dimensions={0}, use_global_device_ids=true | all-gather | bytes 557056 | tf_op jit(solution)/shard_map/all_gather | solution.py:47
  31.7 37.5 %while.30 = (s32[]{:T(128)}, f32[16,128,128]{2,1,0:T(8,128)S(1)}, s32[4]{0:T(128)S(1)}, s32[128]{0:T(128)}, bf16[128,128,128]{2,1,0:T(8,128)(2,1)}, /*index=5*/s...) while((s32[]{:T(128)}, f32[16,128,128]{2,1,0:T(8,128)S(1)}, ...), condition=%wide.region_2.3_spmd, body=%wide.region_0.2_spmd.sunk | while | flops 134743232 | bytes 12588079 | solution.py:33
  70.3 74.0 %reduce-scatter.4.cloned.1.call-done = f32[128,128]{1,0:T(8,128)} async-done(((f32[2048,128]{1,0:T(8,128)}), f32[128,128]{1,0:T(8,128)}) %reduce-scatter.4.cloned.1.call-update) | async-done | bytes 65552 | tf_op jit(solution)/shard_map/reduce_scatter | solution.py:49
  147.2 40.4 %all-gather.3.cloned.1.call-done = bf16[2048,512]{1,0:T(8,128)(2,1)} async-done(((bf16[128,512]{1,0:T(8,128)(2,1)}), bf16[2048,512]{1,0:T(8,128)(2,1)}) %all-gather.3.cloned.1.call-update) | async-done | bytes 2097168 | tf_op jit(solution)/shard_map/all_gather | solution.py:55
  190.1 118.6 %while.31 = (s32[]{:T(128)}, f32[16,128,512]{2,1,0:T(8,128)}, s32[4]{0:T(128)S(1)}, s32[128]{0:T(128)S(1)}, bf16[128,128,128]{2,1,0:T(8,128)(2,1)}, /*index=5*/s...) while((s32[]{:T(128)}, f32[16,128,512]{2,1,0:T(8,128)}, ...), condition=%wide.region_6.7_spmd, body=%wide.region_4.6_spmd.sunk | while | flops 538969280 | bytes 47191088 | solution.py:33
  194.2 7.0 fusion.49
  201.2 18.7 %scatter_fusion.1 = f32[16,128,512]{2,1,0:T(8,128)} fusion(f32[16,128,512]{2,1,0:T(8,128)} %get-tuple-element.369, s32[32]{0:T(128)S(1)} %get-tuple-element.313, f32[32,128,512]{2,1,0:T(8,128)} %fusion.49), kind=kCustom, calls=%fused_computation.4.clone.1 | custom fusion | flops 2097152 | bytes 25165952 | tf_op jit(solution)/shard_map/while/body/eval_jaxpr/scatter-add | solution.py:30
  224.0 7.3 fusion.49
  231.3 18.5 %scatter_fusion.1 = f32[16,128,512]{2,1,0:T(8,128)} fusion(f32[16,128,512]{2,1,0:T(8,128)} %get-tuple-element.369, s32[32]{0:T(128)S(1)} %get-tuple-element.313, f32[32,128,512]{2,1,0:T(8,128)} %fusion.49), kind=kCustom, calls=%fused_computation.4.clone.1 | custom fusion | flops 2097152 | bytes 25165952 | tf_op jit(solution)/shard_map/while/body/eval_jaxpr/scatter-add | solution.py:30
  253.9 7.0 fusion.49
  260.9 18.4 %scatter_fusion.1 = f32[16,128,512]{2,1,0:T(8,128)} fusion(f32[16,128,512]{2,1,0:T(8,128)} %get-tuple-element.369, s32[32]{0:T(128)S(1)} %get-tuple-element.313, f32[32,128,512]{2,1,0:T(8,128)} %fusion.49), kind=kCustom, calls=%fused_computation.4.clone.1 | custom fusion | flops 2097152 | bytes 25165952 | tf_op jit(solution)/shard_map/while/body/eval_jaxpr/scatter-add | solution.py:30
  283.3 7.0 fusion.49
  290.3 18.4 %scatter_fusion.1 = f32[16,128,512]{2,1,0:T(8,128)} fusion(f32[16,128,512]{2,1,0:T(8,128)} %get-tuple-element.369, s32[32]{0:T(128)S(1)} %get-tuple-element.313, f32[32,128,512]{2,1,0:T(8,128)} %fusion.49), kind=kCustom, calls=%fused_computation.4.clone.1 | custom fusion | flops 2097152 | bytes 25165952 | tf_op jit(solution)/shard_map/while/body/eval_jaxpr/scatter-add | solution.py:30
  317.8 148.4 %while.32 = (s32[]{:T(128)}, f32[16,128,512]{2,1,0:T(8,128)}, s32[4]{0:T(128)S(1)}, s32[128]{0:T(128)S(1)}, bf16[128,128,128]{1,2,0:T(8,128)(2,1)}, /*index=5*/s...) while((s32[]{:T(128)}, f32[16,128,512]{2,1,0:T(8,128)}, ...), condition=%wide.region_10.11_spmd, body=%wide.region_8.10_spmd.sunk | while | flops 3223323904 | bytes 59774000 | solution.py:33
  325.7 11.3 %fusion.52 = f32[32,128,512]{2,1,0:T(8,128)} fusion(f32[32,128,512]{2,1,0:T(8,128)} %gather_fusion.2, bf16[128,128,128]{1,2,0:T(8,128)(2,1)} %get-tuple-element.416, s32[]{:T(128)S(6)} %select_n.50), kind=kOutput, calls=%fused_computation.18.clone.1 | convolution fusion | flops 3221225472 | bytes 17825796 | tf_op jit(solution)/shard_map/while/body/eval_jaxpr/tji,tjf->tif/dot_general | solution.py:25
  337.0 18.1 %scatter_fusion.2 = f32[16,128,512]{2,1,0:T(8,128)} fusion(f32[16,128,512]{2,1,0:T(8,128)} %get-tuple-element.402, s32[32]{0:T(128)S(1)} %get-tuple-element.322, f32[32,128,512]{2,1,0:T(8,128)} %fusion.52), kind=kCustom, calls=%fused_computation.5.clone.1 | custom fusion | flops 2097152 | bytes 25165952 | tf_op jit(solution)/shard_map/while/body/eval_jaxpr/scatter-add | solution.py:30
  363.0 11.2 %fusion.52 = f32[32,128,512]{2,1,0:T(8,128)} fusion(f32[32,128,512]{2,1,0:T(8,128)} %gather_fusion.2, bf16[128,128,128]{1,2,0:T(8,128)(2,1)} %get-tuple-element.416, s32[]{:T(128)S(6)} %select_n.50), kind=kOutput, calls=%fused_computation.18.clone.1 | convolution fusion | flops 3221225472 | bytes 17825796 | tf_op jit(solution)/shard_map/while/body/eval_jaxpr/tji,tjf->tif/dot_general | solution.py:25
  374.1 18.1 %scatter_fusion.2 = f32[16,128,512]{2,1,0:T(8,128)} fusion(f32[16,128,512]{2,1,0:T(8,128)} %get-tuple-element.402, s32[32]{0:T(128)S(1)} %get-tuple-element.322, f32[32,128,512]{2,1,0:T(8,128)} %fusion.52), kind=kCustom, calls=%fused_computation.5.clone.1 | custom fusion | flops 2097152 | bytes 25165952 | tf_op jit(solution)/shard_map/while/body/eval_jaxpr/scatter-add | solution.py:30
  400.1 11.2 %fusion.52 = f32[32,128,512]{2,1,0:T(8,128)} fusion(f32[32,128,512]{2,1,0:T(8,128)} %gather_fusion.2, bf16[128,128,128]{1,2,0:T(8,128)(2,1)} %get-tuple-element.416, s32[]{:T(128)S(6)} %select_n.50), kind=kOutput, calls=%fused_computation.18.clone.1 | convolution fusion | flops 3221225472 | bytes 17825796 | tf_op jit(solution)/shard_map/while/body/eval_jaxpr/tji,tjf->tif/dot_general | solution.py:25
  411.3 18.0 %scatter_fusion.2 = f32[16,128,512]{2,1,0:T(8,128)} fusion(f32[16,128,512]{2,1,0:T(8,128)} %get-tuple-element.402, s32[32]{0:T(128)S(1)} %get-tuple-element.322, f32[32,128,512]{2,1,0:T(8,128)} %fusion.52), kind=kCustom, calls=%fused_computation.5.clone.1 | custom fusion | flops 2097152 | bytes 25165952 | tf_op jit(solution)/shard_map/while/body/eval_jaxpr/scatter-add | solution.py:30
  437.1 11.2 %fusion.52 = f32[32,128,512]{2,1,0:T(8,128)} fusion(f32[32,128,512]{2,1,0:T(8,128)} %gather_fusion.2, bf16[128,128,128]{1,2,0:T(8,128)(2,1)} %get-tuple-element.416, s32[]{:T(128)S(6)} %select_n.50), kind=kOutput, calls=%fused_computation.18.clone.1 | convolution fusion | flops 3221225472 | bytes 17825796 | tf_op jit(solution)/shard_map/while/body/eval_jaxpr/tji,tjf->tif/dot_general | solution.py:25
  448.3 17.9 %scatter_fusion.2 = f32[16,128,512]{2,1,0:T(8,128)} fusion(f32[16,128,512]{2,1,0:T(8,128)} %get-tuple-element.402, s32[32]{0:T(128)S(1)} %get-tuple-element.322, f32[32,128,512]{2,1,0:T(8,128)} %fusion.52), kind=kCustom, calls=%fused_computation.5.clone.1 | custom fusion | flops 2097152 | bytes 25165952 | tf_op jit(solution)/shard_map/while/body/eval_jaxpr/scatter-add | solution.py:30
  469.2 55.0 %reduce-scatter.8.cloned.1.call-done = f32[128,512]{1,0:T(8,128)} async-done(((f32[2048,512]{1,0:T(8,128)}), f32[128,512]{1,0:T(8,128)}) %reduce-scatter.8.cloned.1.call-update) | async-done | bytes 262160 | tf_op jit(solution)/shard_map/reduce_scatter | solution.py:63
  528.1 254.6 %all-reduce.3.cloned.1.call-done = (f32[128,512]{1,0:T(8,128)}, f32[512,128]{1,0:T(8,128)}) async-done(((f32[128,512]{1,0:T(8,128)}, f32[512,128]{1,0:T(8,128)}), (f32[128,512]{1,0:T(8,128)}, f32[512,128]{1,0:T(8,128)})) %all-reduce.3.cloned.1.call-update) | async-done | bytes 524304 | tf_op jit(solution)/shard_map/psum | solution.py:68
  (106 shorter events, 103.2 us)
Async XLA Ops:
  7.2 137.2 %copy-start = (bf16[128,512]{1,0:T(8,128)(2,1)S(1)}, bf16[128,512]{1,0:T(8,128)(2,1)}, u32[]{:S(2)}) copy-start(bf16[128,512]{1,0:T(8,128)(2,1)} %param.17) | copy-start | bytes 393220
  7.2 137.2 %reduce-scatter.4.cloned.1.call-start = ((), (), s32[]{:S(2)}) async-start(), calls=%async_computation.3 | async-start | bytes 1114112 | tf_op jit(solution)/shard_map/reduce_scatter | solution.py:49
  31.7 114.4 %copy-start.3 = (bf16[512,128]{1,0:T(8,128)(2,1)S(1)}, bf16[512,128]{1,0:T(8,128)(2,1)}, u32[]{:S(2)}) copy-start(bf16[512,128]{1,0:T(8,128)(2,1)} %param.18) | copy-start | bytes 393220
  31.7 114.4 %copy-start.5 = (bf16[128,128]{1,0:T(8,128)(2,1)S(1)}, bf16[128,128]{1,0:T(8,128)(2,1)}, u32[]{:S(2)}) copy-start(bf16[128,128]{1,0:T(8,128)(2,1)} %param.19) | copy-start | bytes 98308
  69.2 1.0 copy-start.2
  69.2 120.8 %copy-start.7 = (s32[128]{0:T(128)S(1)}, s32[128]{0:T(128)}, u32[]{:S(2)}) copy-start(s32[128]{0:T(128)} %get-tuple-element.456) | copy-start | bytes 1540
  69.3 120.8 %copy-start.8 = (s32[128]{0:T(128)S(1)}, s32[128]{0:T(128)}, u32[]{:S(2)}) copy-start(s32[128]{0:T(128)} %get-tuple-element.458) | copy-start | bytes 1540
  70.2 117.3 %all-gather.3.cloned.1.call-start = ((), (), s32[]{:S(2)}) async-start(), calls=%async_computation.4 | async-start | bytes 2228224 | tf_op jit(solution)/shard_map/all_gather | solution.py:55
  146.1 169.3 %all-gather.5.cloned.1.call-start = ((), (), s32[]{:S(2)}) async-start(), calls=%async_computation.6 | async-start | bytes 4456448 | tf_op jit(solution)/shard_map/all_gather | solution.py:61
  147.1 319.2 %reduce-scatter.6.cloned.1.call-start = ((), (), s32[]{:S(2)}) async-start(), calls=%async_computation.5 | async-start | bytes 4456448 | tf_op jit(solution)/shard_map/reduce_scatter | solution.py:57
  187.5 2.5 copy-start.1
  308.7 215.5 %reduce-scatter.8.cloned.1.call-start = ((), (), s32[]{:S(2)}) async-start(), calls=%async_computation.7 | async-start | bytes 4456448 | tf_op jit(solution)/shard_map/reduce_scatter | solution.py:63
  466.2 0.8 copy-start.6
  466.2 58.0 %copy-start.9 = (f32[128,128]{1,0:T(8,128)S(1)}, f32[128,128]{1,0:T(8,128)}, u32[]{:S(2)}) copy-start(f32[128,128]{1,0:T(8,128)} %reduce-scatter.4.cloned.1.call-done) | copy-start | bytes 196612
  466.2 58.0 %copy-start.10 = (f32[128,512]{1,0:T(8,128)S(1)}, f32[128,512]{1,0:T(8,128)}, u32[]{:S(2)}) copy-start(f32[128,512]{1,0:T(8,128)} %get-tuple-element.182) | copy-start | bytes 786436
  466.2 60.1 %copy-start.4 = (bf16[512,128]{1,0:T(8,128)(2,1)S(1)}, bf16[512,128]{1,0:T(8,128)(2,1)}, u32[]{:S(2)}) copy-start(bf16[512,128]{1,0:T(8,128)(2,1)} %param.18) | copy-start | bytes 393220
  466.2 316.5 %all-reduce.3.cloned.1.call-start = ((), (), s32[]{:S(2)}) async-start(), calls=%async_computation.8 | async-start | bytes 1048576 | tf_op jit(solution)/shard_map/psum | solution.py:68
Sparse Core Ops, SparseCore 0:
  70.4 73.9 reduce-scatter.3
  146.3 41.1 all-gather.2
  190.8 54.4 all-gather.4
  308.8 78.8 reduce-scatter.5
  466.4 57.7 reduce-scatter.7
  530.2 252.4 all-reduce.2
where the time goes:
time: 795 us; the launch traced here: 793 us
  waiting for transfers between devices  424 us (53%)
  other arithmetic  160 us (20%)
  matrix products  89.7 us (11%)
  local copies, waits for them, and re-layouts  71.7 us (9%)
  blocking collectives  24.4 us (3%)
  between operations  14.2 us (2%)
  loops' own time  7.95 us (1%)
    psum x1, waiting for transfers between devices, on_device(): w_in_grad, w_out_grad = lax.psum((in_term, out_term), ('row', 'col'))  255 us
    scatter-add x12, other arithmetic, add_block(): return (totals.at[target].add(product), None)  157 us
    reduce_scatter x1, waiting for transfers between devices, on_device(): lax.psum_scatter(partial_in, 'col', scatter_dimension=0, tiled=True)  74 us
    reduce_scatter x1, waiting for transfers between devices, on_device(): lax.psum_scatter(partial_grad, 'row', scatter_dimension=0, tiled=True)  55 us
    gather x12, local copies, waits for them, and re-layouts, add_block(): picked = blocks[source]  48.1 us
    dot_general x4, matrix products, add_block(): jnp.einsum(pattern, chosen.astype(jnp.float32), picked, precision=lax.Pre...  44.8 us
    all_gather x1, waiting for transfers between devices, on_device(): gathered_hid = lax.all_gather(hidden, 'row', axis=0, tiled=True)  40.4 us
    dot_general x8, matrix products, add_block(): jnp.einsum(pattern, chosen, picked, preferred_element_type=jnp.float32)  36.1 us
  transfers between devices with their start and end apart: 6, of which 4 were waited for; matrix products, arithmetic and copies ran while one was open for 35% of the time, Pallas kernels for 0%

commit v1 on v0

v1 whole, which is shorter than its diff:
```python
import functools
import math

import jax
import jax.numpy as jnp
from jax import lax
from jax.experimental import pallas as pl
from jax.experimental.pallas import tpu as pltpu
from jax.sharding import PartitionSpec as P

B, F = jnp.bfloat16, jnp.float32
VMEM = pl.BlockSpec(memory_space=pltpu.VMEM)
SMEM = pl.BlockSpec(memory_space=pltpu.SMEM)
T = 128
G = 16
UNROLL = 32


def kernel_call(body, out, specs, scratch, flops, name):
    return pl.pallas_call(
        body,
        out_shape=out,
        in_specs=specs,
        out_specs=jax.tree.map(lambda _: VMEM, out),
        scratch_shapes=scratch,
        cost_estimate=pl.CostEstimate(flops=flops, bytes_accessed=6 << 20, transcendentals=0),
        compiler_params=pltpu.CompilerParams(vmem_limit_bytes=40 << 20),
        name=name,
    )


def each_tile(total, count, product, target):
    def step(block, carry):
        first = block * UNROLL
        parts = [product(first + u) for u in range(UNROLL)]
        for u in range(UNROLL):
            total[target(first + u)] += parts[u]
        return carry

    lax.fori_loop(0, count // UNROLL, step, 0)


def spread_first(rows, cols, tiles, feats, grads, out, total):
    total[...] = jnp.zeros_like(total)
    each_tile(
        total,
        tiles.shape[0],
        lambda k: jnp.dot(tiles[k], feats[cols[k]], preferred_element_type=F),
        lambda k: rows[k],
    )
    for i in range(G):
        value = total[i]
        high = value.astype(B)
        out[i, 0:T] = high
        out[i, T : 2 * T] = (value - high.astype(F)).astype(B)
        out[i, 2 * T : 3 * T] = grads[...]


def spread_second(rows, cols, tiles, feats, out, total):
    total[...] = jnp.zeros_like(total)
    each_tile(
        total,
        tiles.shape[0],
        lambda k: jnp.dot(tiles[k], feats[cols[k]], preferred_element_type=F),
        lambda k: rows[k],
    )
    for i in range(G):
        out[i, 0:T] = total[i].astype(B)
        out[i, T:] = jnp.zeros((out.shape[1] - T, T), B)


def spread_back(rows, cols, tiles, received, out, turned):
    for i in range(G):
        turned[i] = received[i, 2 * T : 3 * T].T
    out[...] = jnp.zeros_like(out)
    each_tile(
        out,
        tiles.shape[0],
        lambda k: jnp.dot(turned[rows[k]], tiles[k], preferred_element_type=F),
        lambda k: cols[k],
    )


def dense_part(scale, agg, pulled, w_in, w_out, w_out_t, proj, packed, in_sum, out_sum):
    in_sum[...] = jnp.zeros_like(in_sum)
    out_sum[...] = jnp.zeros_like(out_sum)

    def step(q, carry):
        nodes = agg[q]
        pre = jnp.dot(nodes, w_in[...], preferred_element_type=F)
        sig = jax.nn.sigmoid(pre)
        act = pre * sig
        hidden = act.astype(B)
        proj[q] = jnp.dot(hidden, w_out[...], preferred_element_type=F).astype(B)
        back = (pulled[q] * scale).astype(B)
        grad = lax.dot_general(
            back, w_out_t[...], (((0,), (0,)), ((), ())), preferred_element_type=F
        )
        grad_pre = grad * sig * (1.0 + pre * (1.0 - sig))
        in_sum[...] += lax.dot_general(
            nodes, grad_pre.astype(B), (((0,), (0,)), ((), ())), preferred_element_type=F
        )
        out_sum[...] += jnp.dot(back, hidden, preferred_element_type=F)
        return carry

    lax.fori_loop(0, G, step, 0)
    out_grad = out_sum[...].T
    for s in range(G):
        parts = [in_sum[8 * s : 8 * s + 8, T * b : T * b + T] for b in range(4)]
        parts.append(out_grad[32 * s : 32 * s + 32])
        packed[s] = jnp.concatenate(parts, 0).astype(B)


def unpack(slices, in_grad, out_grad):
    for s in range(G):
        piece = slices[s % 2, s // 2].astype(F)
        for b in range(4):
            in_grad[8 * s : 8 * s + 8, T * b : T * b + T] = piece[8 * b : 8 * b + 8]
        out_grad[32 * s : 32 * s + 32] = piece[32:64]


def swap(value, axis, groups=None):
    return lax.all_to_all(value, axis, 0, 0, tiled=True, axis_index_groups=groups)


def gather_row(value):
    same_core = [[2 * z + core for z in range(G // 2)] for core in range(2)]
    same_chip = [[2 * z, 2 * z + 1] for z in range(G // 2)]
    along_z = swap(jnp.broadcast_to(value[None], (G // 2,) + value.shape), "row", same_core)
    return lax.all_gather(along_z, "row", axis=0, axis_index_groups=same_chip)


def on_device(node_input, adj_tiles, tile_row, tile_col, weight_in, weight_out, logit_grad):
    tiles = adj_tiles.reshape(-1, T, T)
    rows = tile_row.reshape(-1)
    cols = tile_col.reshape(-1)
    cols = (cols % 2) * (G // 2) + cols // 2
    node_total = node_input.shape[0] * G * G
    scale = 1.0 / math.sqrt(node_total)
    spread_flops = 2 * tiles.shape[0] * T**3
    sds = jax.ShapeDtypeStruct

    x_all = gather_row(node_input).reshape(G, T, T)
    first = kernel_call(
        spread_first, sds((G, 3 * T, T), B), [SMEM, SMEM, VMEM, VMEM, VMEM],
        [pltpu.VMEM((G, T, T), F)], spread_flops, "spread_first",
    )(rows, cols, tiles, x_all, logit_grad)
    received = swap(first, "col")
    sums = received[:, : 2 * T].astype(F)
    agg_in = (sums[:, :T] + sums[:, T:]).sum(0).astype(B)

    agg_all = gather_row(agg_in).reshape(G, T, T)
    pulled = kernel_call(
        spread_back, sds((G, T, T), F), [SMEM, SMEM, VMEM, VMEM],
        [pltpu.VMEM((G, T, T), B)], spread_flops, "spread_back",
    )(rows, cols, tiles, received)

    width = weight_in.shape[1]
    proj, packed = kernel_call(
        functools.partial(dense_part, scale), (sds((G, T, T), B), sds((G, 64, T), B)), [VMEM] * 5,
        [pltpu.VMEM((T, width), F), pltpu.VMEM((T, width), F)], 10 * G * T * T * width, "dense_part",
    )(agg_all, pulled, weight_in, weight_out, weight_out.T)

    packed = swap(packed, "row")
    second = kernel_call(
        spread_second, sds((G, T + 64, T), B), [SMEM, SMEM, VMEM, VMEM],
        [pltpu.VMEM((G, T, T), F)], spread_flops, "spread_second",
    )(rows, cols, tiles, proj)
    row_sum = packed.astype(F).sum(0).astype(B)
    second = second.at[:, T:].set(jnp.broadcast_to(row_sum[None], (G, 64, T)))
    second = swap(second, "col").astype(F).sum(0)
    logits = second[:T]

    slices = gather_row(second[T:].astype(B))
    w_in_grad, w_out_grad = kernel_call(
        unpack, (sds((T, width), F), sds((width, T), F)), [VMEM], [], 0, "unpack",
    )(slices)
    return (logits, w_in_grad, w_out_grad)


def solution(mesh):
    placed = (
        P(("row", "col"), None),
        P("row", "col", None, None, None),
        P("row", "col", None),
        P("row", "col", None),
        P(),
        P(),
        P(("row", "col"), None),
    )
    return jax.shard_map(
        on_device,
        mesh=mesh,
        in_specs=placed,
        out_specs=(P(("row", "col"), None), P(), P()),
        check_vma=False,
    )
```

time: 795 us -> 141 us (0.18)
  waiting for transfers between devices: 424 us -> 28.5 us
  other arithmetic: 160 us -> 1.12 us
  matrix products: 89.7 us -> 0 us
  local copies, waits for them, and re-layouts: 71.7 us -> 11.7 us
  blocking collectives: 24.4 us -> 59.7 us
  Pallas kernels: 0 us -> 19.1 us
  starting transfers between devices: 0.43 us -> 19.5 us
  between operations: 14.2 us -> 0.76 us
  loops' own time: 7.95 us -> 0 us
    psum x1 -> x0, waiting for transfers between devices: 255 us -> none  [on_device(): w_in_grad, w_out_grad = lax.psum((in_term, out_term), ('row', 'col'))]
    scatter-add x12 -> x0, other arithmetic: 157 us -> none  [add_block(): return (totals.at[target].add(product), None)]
    reduce_scatter x3 -> x0, waiting for transfers between devices: 129 us -> none  [the longest x1 74 us: on_device(): lax.psum_scatter(partial_in, 'col', scatter_dimension=0, tiled=True)]
    dot_general x17 -> x0, matrix products: 89.7 us -> none  [the longest x4 44.8 us: add_block(): jnp.einsum(pattern, chosen.astype(jnp.float32), picked, precision=lax.Pre...]
    gather x12 -> x0, local copies, waits for them, and re-layouts: 48.1 us -> none  [add_block(): picked = blocks[source]]
    all_to_all x0 -> x2, blocking collectives: none -> 46.9 us  [swap(): lax.all_to_all(value, axis, 0, 0, tiled=True, axis_index_groups=groups)]
    all_gather x2 -> x0, waiting for transfers between devices: 40.4 us -> none  [the longest x1 40.4 us: on_device(): gathered_hid = lax.all_gather(hidden, 'row', axis=0, tiled=True)]
    all_to_all x0 -> x4, waiting for transfers between devices: none -> 28.5 us  [swap(): lax.all_to_all(value, axis, 0, 0, tiled=True, axis_index_groups=groups)]
  transfers between devices with their start and end apart: 6 -> 4, of which waited for: 4 -> 4; matrix products, arithmetic and copies ran while one was open for 35% -> 1% of each run, Pallas kernels for 0% -> 4%
where the time goes in v1:
time: 141 us; the launch traced here: 140 us
  blocking collectives  59.7 us (42%)
  waiting for transfers between devices  28.5 us (20%)
  starting transfers between devices  19.5 us (14%)
  Pallas kernels  19.1 us (14%)
  local copies, waits for them, and re-layouts  11.7 us (8%)
    all_to_all x2, blocking collectives, swap(): lax.all_to_all(value, axis, 0, 0, tiled=True, axis_index_groups=groups)  46.9 us
    all_to_all x4, waiting for transfers between devices, swap(): lax.all_to_all(value, axis, 0, 0, tiled=True, axis_index_groups=groups)  28.5 us
    all_to_all x4, starting transfers between devices, swap(): lax.all_to_all(value, axis, 0, 0, tiled=True, axis_index_groups=groups)  19.5 us
    all_gather x3, blocking collectives, gather_row(): return lax.all_gather(along_z, 'row', axis=0, axis_index_groups=same_chip)  12.8 us
    pallas_call x1, Pallas kernels, on_device(): kernel_call(functools.partial(dense_part, scale), (sds((G, T, T), B), sds...  10.3 us
    unnamed x17, local copies, waits for them, and re-layouts  8.1 us
    broadcast_in_dim x3, local copies, waits for them, and re-layouts, gather_row(): jnp.broadcast_to(value[None], (G // 2,) + value.shape)  2.91 us
  transfers between devices with their start and end apart: 4, of which 4 were waited for; matrix products, arithmetic and copies ran while one was open for 1% of the time, Pallas kernels for 4%

profile of v1, /device:TPU:1, one launch (start us, length us, event | category | flops | bytes accessed | tf_op | source)
XLA Modules:
  0.0 140.5 jit_solution(1339810107848172201)
XLA Ops:
  0.6 1.5 %broadcast_in_dim.6 = bf16[8,128,128]{2,1,0:T(8,128)(2,1)} broadcast(bf16[128,128]{1,0:T(8,128)(2,1)} %param.9), dimensions={1,2} | broadcast | bytes 294912 | tf_op jit(solution)/shard_map/broadcast_in_dim | solution.py:129
  2.1 9.0 %all-to-all-start = ((bf16[8,128,128]{2,1,0:T(8,128)(2,1)}), bf16[8,128,128]{2,1,0:T(8,128)(2,1)S(1)}, u32[]{:S(2)}, u32[]{:S(2)}) async-start(bf16[8,128,128]{2,1,0:T(8,128)(2,1)} %broadcast_in_dim.6), calls=%async_computation | async-start | bytes 524288 | tf_op jit(solution)/shard_map/all_to_all | solution.py:123
  11.8 9.7 %all-to-all-done = bf16[8,128,128]{2,1,0:T(8,128)(2,1)S(1)} async-done(((bf16[8,128,128]{2,1,0:T(8,128)(2,1)}), bf16[8,128,128]{2,1,0:T(8,128)(2,1)S(1)}, u32[]{:S(2)}, u32[]{:S(2)}) %all-to-all-start) | async-done | bytes 262176 | tf_op jit(solution)/shard_map/all_to_all | solution.py:123
  21.5 4.3 %all-gather.feats = bf16[16,128,128]{2,1,0:T(8,128)(2,1)S(1)} all-gather(bf16[8,128,128]{2,1,0:T(8,128)(2,1)S(1)} %all-to-all-done), channel_id=2, replica_groups={{0,16},{32,48},{64,80},{96,112},{128,144},{160,176},{192,208},{224,240}..., dimensions={0}, use_global_device_ids=true | all-gather | bytes 786432 | tf_op jit(solution)/shard_map/all_gather | solution.py:130
  25.8 2.2 %copy-done = bf16[1,1,128,128,128]{4,3,2,1,0:T(8,128)(2,1)S(1)} copy-done((bf16[1,1,128,128,128]{4,3,2,1,0:T(8,128)(2,1)S(1)}, bf16[1,1,128,128,128]{4,3,2,1,0:T(8,128)(2,1)}, u32[]{:S(2)}) %copy-start) | copy-done | bytes 4194328
  28.0 0.8 copy-done.4
  29.4 2.7 %spread_first.1 = bf16[16,384,128]{2,1,0:T(8,128)(2,1)S(1)} custom-call(s32[128]{0:T(128)S(1)} %bitcast.22, s32[128]{0:T(128)S(1)} %fusion.2.cols, bf16[128,128,128]{2,1,0:T(8,128)(2,1)S(1)} %bitcast.17, bf16[16,128,128]{2,1,0:T(8,128)(2,1)S(1)} %all-gather.feats, bf16[128,128]{1,0:T(8,128)(2,1)S(1)} %copy-done.4), custom_call_target="tpu_custom_call" | custom-call | flops 536870912 | bytes 6291456 | tf_op jit(solution)/shard_map/spread_first/pallas_call | solution.py:144
  32.1 28.5 %all_to_all.30.received = bf16[16,384,128]{2,1,0:T(8,128)(2,1)S(1)} all-to-all(bf16[16,384,128]{2,1,0:T(8,128)(2,1)S(1)} %spread_first.1), channel_id=1, replica_groups=mesh['row'=16,'col'=16] {'col'}, dimensions={0} | all-to-all | bytes 3145728 | tf_op jit(solution)/shard_map/all_to_all | solution.py:123
  60.9 0.7 broadcast_in_dim.7
  61.7 3.4 %all-to-all-start.2 = ((bf16[8,128,128]{2,1,0:T(8,128)(2,1)}), bf16[8,128,128]{2,1,0:T(8,128)(2,1)S(1)}, u32[]{:S(2)}, u32[]{:S(2)}) async-start(bf16[8,128,128]{2,1,0:T(8,128)(2,1)} %broadcast_in_dim.7), calls=%async_computation.2 | async-start | bytes 524288 | tf_op jit(solution)/shard_map/all_to_all | solution.py:123
  65.2 2.2 %copy-done.1 = bf16[1,1,128,128,128]{4,3,2,1,0:T(8,128)(2,1)S(1)} copy-done((bf16[1,1,128,128,128]{4,3,2,1,0:T(8,128)(2,1)S(1)}, bf16[1,1,128,128,128]{4,3,2,1,0:T(8,128)(2,1)}, u32[]{:S(2)}) %copy-start.1) | copy-done | bytes 4194328
  67.4 2.7 %spread_back.1.pulled = f32[16,128,128]{2,1,0:T(8,128)S(1)} custom-call(s32[128]{0:T(128)S(1)} %bitcast.23, s32[128]{0:T(128)S(1)} %fusion.2.cols, bf16[128,128,128]{2,1,0:T(8,128)(2,1)S(1)} %bitcast.18, bf16[16,384,128]{2,1,0:T(8,128)(2,1)S(1)} %all_to_all.30.received), custom_call_target="tpu_custom_call" | custom-call | flops 536870912 | bytes 6291456 | tf_op jit(solution)/shard_map/spread_back/pallas_call | solution.py:153
  70.2 4.4 %all-to-all-done.2 = bf16[8,128,128]{2,1,0:T(8,128)(2,1)S(1)} async-done(((bf16[8,128,128]{2,1,0:T(8,128)(2,1)}), bf16[8,128,128]{2,1,0:T(8,128)(2,1)S(1)}, u32[]{:S(2)}, u32[]{:S(2)}) %all-to-all-start.2) | async-done | bytes 262176 | tf_op jit(solution)/shard_map/all_to_all | solution.py:123
  74.6 5.1 %all-gather.1.agg = bf16[16,128,128]{2,1,0:T(8,128)(2,1)S(1)} all-gather(bf16[8,128,128]{2,1,0:T(8,128)(2,1)S(1)} %all-to-all-done.2), channel_id=3, replica_groups={{0,16},{32,48},{64,80},{96,112},{128,144},{160,176},{192,208},{224,240}..., dimensions={0}, use_global_device_ids=true | all-gather | bytes 786432 | tf_op jit(solution)/shard_map/all_gather | solution.py:130
  79.6 10.3 %dense_part.1 = (bf16[16,128,128]{2,1,0:T(8,128)(2,1)S(1)}, bf16[16,64,128]{2,1,0:T(8,128)(2,1)}) custom-call(bf16[16,128,128]{2,1,0:T(8,128)(2,1)S(1)} %all-gather.1.agg, f32[16,128,128]{2,1,0:T(8,128)S(1)} %spread_back.1.pulled, bf16[128,512]{1,0:T(8,128)(2,1)S(1)} %copy-done.7, bf16[512,128]{1,0:T(8,128)(2,1)S(1)} %copy-done.3, bf16[128,512]{1,0:T(8,128)(2,1)S(1)} %bitcast.21), custom_call_target="tpu_custom_call" | custom-call | flops 1342177280 | bytes 6291456 | tf_op jit(solution)/shard_map/dense_part/pallas_call | solution.py:159
  89.9 3.7 %all-to-all-start.3 = ((bf16[16,64,128]{2,1,0:T(8,128)(2,1)}), bf16[16,64,128]{2,1,0:T(8,128)(2,1)S(1)}, u32[]{:S(2)}, u32[]{:S(2)}) async-start(bf16[16,64,128]{2,1,0:T(8,128)(2,1)} %get-tuple-element.20), calls=%async_computation.3 | async-start | bytes 524288 | tf_op jit(solution)/shard_map/all_to_all | solution.py:123
  93.6 2.2 %copy-done.2 = bf16[1,1,128,128,128]{4,3,2,1,0:T(8,128)(2,1)S(1)} copy-done((bf16[1,1,128,128,128]{4,3,2,1,0:T(8,128)(2,1)S(1)}, bf16[1,1,128,128,128]{4,3,2,1,0:T(8,128)(2,1)}, u32[]{:S(2)}) %copy-start.2) | copy-done | bytes 4194328
  95.8 2.6 %spread_second.1 = bf16[16,192,128]{2,1,0:T(8,128)(2,1)S(1)} custom-call(s32[128]{0:T(128)S(1)} %bitcast.24, s32[128]{0:T(128)S(1)} %fusion.2.cols, bf16[128,128,128]{2,1,0:T(8,128)(2,1)S(1)} %bitcast.19, bf16[16,128,128]{2,1,0:T(8,128)(2,1)S(1)} %get-tuple-element.19.feats), custom_call_target="tpu_custom_call" | custom-call | flops 536870912 | bytes 6291456 | tf_op jit(solution)/shard_map/spread_second/pallas_call | solution.py:165
  98.4 7.0 %all-to-all-done.3 = bf16[16,64,128]{2,1,0:T(8,128)(2,1)S(1)} async-done(((bf16[16,64,128]{2,1,0:T(8,128)(2,1)}), bf16[16,64,128]{2,1,0:T(8,128)(2,1)S(1)}, u32[]{:S(2)}, u32[]{:S(2)}) %all-to-all-start.3) | async-done | bytes 262176 | tf_op jit(solution)/shard_map/all_to_all | solution.py:123
  105.6 18.4 %all_to_all.31 = bf16[16,192,128]{2,1,0:T(8,128)(2,1)S(1)} all-to-all(bf16[16,192,128]{2,1,0:T(8,128)(2,1)S(1)} %broadcast_dynamic-update-slice_fusion), channel_id=1, replica_groups=mesh['row'=16,'col'=16] {'col'}, dimensions={0} | all-to-all | bytes 1572864 | tf_op jit(solution)/shard_map/all_to_all | solution.py:123
  124.7 3.4 %all-to-all-start.5 = ((bf16[8,64,128]{2,1,0:T(8,128)(2,1)}), bf16[8,64,128]{2,1,0:T(8,128)(2,1)S(1)}, u32[]{:S(2)}, u32[]{:S(2)}) async-start(bf16[8,64,128]{2,1,0:T(8,128)(2,1)} %broadcast_in_dim.8), calls=%async_computation.5 | async-start | bytes 262144 | tf_op jit(solution)/shard_map/all_to_all | solution.py:123
  128.8 7.4 %all-to-all-done.5 = bf16[8,64,128]{2,1,0:T(8,128)(2,1)S(1)} async-done(((bf16[8,64,128]{2,1,0:T(8,128)(2,1)}), bf16[8,64,128]{2,1,0:T(8,128)(2,1)S(1)}, u32[]{:S(2)}, u32[]{:S(2)}) %all-to-all-start.5) | async-done | bytes 131104 | tf_op jit(solution)/shard_map/all_to_all | solution.py:123
  136.2 3.5 %all-gather.2 = bf16[16,64,128]{2,1,0:T(8,128)(2,1)S(1)} all-gather(bf16[8,64,128]{2,1,0:T(8,128)(2,1)S(1)} %all-to-all-done.5), channel_id=4, replica_groups={{0,16},{32,48},{64,80},{96,112},{128,144},{160,176},{192,208},{224,240}..., dimensions={0}, use_global_device_ids=true | all-gather | bytes 393216 | tf_op jit(solution)/shard_map/all_gather | solution.py:130
  139.7 0.8 unpack.1
  (22 shorter events, 3.3 us)
Async XLA Ops:
  2.1 19.4 %all-to-all-start = ((bf16[8,128,128]{2,1,0:T(8,128)(2,1)}), bf16[8,128,128]{2,1,0:T(8,128)(2,1)S(1)}, u32[]{:S(2)}, u32[]{:S(2)}) async-start(bf16[8,128,128]{2,1,0:T(8,128)(2,1)} %broadcast_in_dim.6), calls=%async_computation | async-start | bytes 524288 | tf_op jit(solution)/shard_map/all_to_all | solution.py:123
  25.8 2.2 %copy-start = (bf16[1,1,128,128,128]{4,3,2,1,0:T(8,128)(2,1)S(1)}, bf16[1,1,128,128,128]{4,3,2,1,0:T(8,128)(2,1)}, u32[]{:S(2)}) copy-start(bf16[1,1,128,128,128]{4,3,2,1,0:T(8,128)(2,1)} %param.10) | copy-start | bytes 12582916
  28.0 0.8 copy-start.4
  28.7 0.7 copy-start.5
  60.8 4.3 %copy-start.3 = (bf16[512,128]{1,0:T(8,128)(2,1)S(1)}, bf16[512,128]{1,0:T(8,128)(2,1)}, u32[]{:S(2)}) copy-start(bf16[512,128]{1,0:T(8,128)(2,1)} %w_out.1) | copy-start | bytes 393220
  60.8 4.4 %copy-start.6 = (s32[1,1,128]{2,1,0:T(1,128)S(1)}, s32[1,1,128]{2,1,0:T(1,128)}, u32[]{:S(2)}) copy-start(s32[1,1,128]{2,1,0:T(1,128)} %param.11) | copy-start | bytes 1540
  61.7 12.9 %all-to-all-start.2 = ((bf16[8,128,128]{2,1,0:T(8,128)(2,1)}), bf16[8,128,128]{2,1,0:T(8,128)(2,1)S(1)}, u32[]{:S(2)}, u32[]{:S(2)}) async-start(bf16[8,128,128]{2,1,0:T(8,128)(2,1)} %broadcast_in_dim.7), calls=%async_computation.2 | async-start | bytes 524288 | tf_op jit(solution)/shard_map/all_to_all | solution.py:123
  65.2 2.2 %copy-start.1 = (bf16[1,1,128,128,128]{4,3,2,1,0:T(8,128)(2,1)S(1)}, bf16[1,1,128,128,128]{4,3,2,1,0:T(8,128)(2,1)}, u32[]{:S(2)}) copy-start(bf16[1,1,128,128,128]{4,3,2,1,0:T(8,128)(2,1)} %param.10) | copy-start | bytes 12582916
  67.4 12.2 %copy-start.7 = (bf16[128,512]{1,0:T(8,128)(2,1)S(1)}, bf16[128,512]{1,0:T(8,128)(2,1)}, u32[]{:S(2)}) copy-start(bf16[128,512]{1,0:T(8,128)(2,1)} %w_in.1) | copy-start | bytes 393220
  89.9 15.6 %all-to-all-start.3 = ((bf16[16,64,128]{2,1,0:T(8,128)(2,1)}), bf16[16,64,128]{2,1,0:T(8,128)(2,1)S(1)}, u32[]{:S(2)}, u32[]{:S(2)}) async-start(bf16[16,64,128]{2,1,0:T(8,128)(2,1)} %get-tuple-element.20), calls=%async_computation.3 | async-start | bytes 524288 | tf_op jit(solution)/shard_map/all_to_all | solution.py:123
  93.6 2.2 %copy-start.2 = (bf16[1,1,128,128,128]{4,3,2,1,0:T(8,128)(2,1)S(1)}, bf16[1,1,128,128,128]{4,3,2,1,0:T(8,128)(2,1)}, u32[]{:S(2)}) copy-start(bf16[1,1,128,128,128]{4,3,2,1,0:T(8,128)(2,1)} %param.10) | copy-start | bytes 12582916
  124.7 11.4 %all-to-all-start.5 = ((bf16[8,64,128]{2,1,0:T(8,128)(2,1)}), bf16[8,64,128]{2,1,0:T(8,128)(2,1)S(1)}, u32[]{:S(2)}, u32[]{:S(2)}) async-start(bf16[8,64,128]{2,1,0:T(8,128)(2,1)} %broadcast_in_dim.8), calls=%async_computation.5 | async-start | bytes 262144 | tf_op jit(solution)/shard_map/all_to_all | solution.py:123

commit v2 on v0

v2 whole, which is shorter than its diff:
```python
import functools
import math

import jax
import jax.numpy as jnp
from jax import lax
from jax.experimental import pallas as pl
from jax.experimental.pallas import tpu as pltpu
from jax.sharding import PartitionSpec as P

B, F = jnp.bfloat16, jnp.float32
VMEM = pl.BlockSpec(memory_space=pltpu.VMEM)
SMEM = pl.BlockSpec(memory_space=pltpu.SMEM)
ANY = pl.BlockSpec(memory_space=pl.ANY)
T = 128
G = 16
Z = 8
S = 32
UNROLL = 32
DENSE_UNROLL = 4


def kernel_call(body, name, flops, out, specs, scratch=(), limit=20):
    return pl.pallas_call(
        body,
        out_shape=out,
        in_specs=specs,
        out_specs=jax.tree.map(lambda _: VMEM, out),
        scratch_shapes=list(scratch),
        cost_estimate=pl.CostEstimate(flops=flops, bytes_accessed=6 << 20, transcendentals=0),
        compiler_params=pltpu.CompilerParams(vmem_limit_bytes=limit << 20),
        name=name,
    )


def fetch(pairs, sems):
    copies = [pltpu.make_async_copy(a, b, sems.at[i]) for i, (a, b) in enumerate(pairs)]
    for copy in copies:
        copy.start()
    return copies


def each_tile(tiles, held, sems, total, before, product, target):
    steps = tiles.shape[0] // UNROLL
    parts = [pl.ds(step * UNROLL, UNROLL) for step in range(steps)]
    arrivals = fetch([(tiles.at[part], held.at[part]) for part in parts], sems)
    total[...] = jnp.zeros_like(total)
    before()
    for step in range(steps):
        arrivals[step].wait()
        first = step * UNROLL
        terms = [product(held[first + u], first + u) for u in range(UNROLL)]
        for u in range(UNROLL):
            total[target(first + u)] += terms[u]


def spread_first(rows, cols, tiles, feats, grads, out, held, sems, ids, more, own, total):
    copies = fetch([(rows, ids.at[0]), (cols, ids.at[1]), (grads, own)], more)

    def before():
        for copy in copies:
            copy.wait()

    each_tile(
        tiles,
        held,
        sems,
        total,
        before,
        lambda tile, k: jnp.dot(tile, feats[ids[1, k]], preferred_element_type=F),
        lambda k: ids[0, k],
    )
    for i in range(G):
        out[i, 0:T] = total[i].astype(B)
        out[i, T:] = own[...]


def spread_second(rows, cols, tiles, high, low, out, held, sems, ids, more, total):
    copies = fetch([(rows, ids.at[0]), (cols, ids.at[1])], more)

    def before():
        for copy in copies:
            copy.wait()

    def product(tile, k):
        q = ids[1, k]
        twice = jnp.concatenate([tile, tile], 1)
        feats = jnp.concatenate([part[q & 1, q >> 1] for part in (high, low)], 0)
        return jnp.dot(twice, feats, preferred_element_type=F)

    each_tile(tiles, held, sems, total, before, product, lambda k: ids[0, k])
    for i in range(G):
        out[i, 0:T] = total[i].astype(B)
        out[i, T:] = jnp.zeros((S, T), B)


def spread_back(core, rows, cols, tiles, received, keep, send, held, sems, ids, more, turned, total):
    copies = fetch([(rows, ids.at[0]), (cols, ids.at[1])], more)

    def before():
        for i in range(G):
            turned[i] = received[i, T:].T
        for copy in copies:
            copy.wait()

    def target(k):
        q = ids[1, k]
        return ((q & 1) ^ core[0]) * Z + (q >> 1)

    each_tile(
        tiles,
        held,
        sems,
        total,
        before,
        lambda tile, k: jnp.dot(turned[ids[0, k]], tile, preferred_element_type=F),
        target,
    )
    keep[...] = total[:Z]
    send[...] = total[Z:].astype(B)


def collect(received, out):
    total = jnp.zeros((T, T), F)
    for i in range(G):
        total = total + received[i, 0:T].astype(F)
    total = total.astype(B)
    for z in range(Z):
        out[z] = total


def halves(value):
    high = value.astype(B)
    return high, (value - high.astype(F)).astype(B)


def product(left, right, dims=((1,), (0,))):
    return lax.dot_general(left, right, (dims, ((), ())), preferred_element_type=F)


def dense(scale, core, agg, keep, got, w_in, w_out, *refs):
    *proj, own, other, in_sum, out_sum = refs
    in_sum[...] = jnp.zeros_like(in_sum)
    out_sum[...] = jnp.zeros_like(out_sum)
    turned = w_out[...].T
    turned = jnp.concatenate([turned, turned], 0)

    def two_tiles(p):
        nodes = agg[p]
        pre = product(nodes, w_in[...])
        sig = jax.nn.sigmoid(pre)
        act = pre * sig
        high, low = halves(act)
        projected = halves(product(high, w_out[...]) + product(low, w_out[...]))
        for i in range(2):
            for part in range(2):
                proj[part][2 * p + i] = projected[part][i * T : i * T + T]
        pulled = [(keep[2 * p + i] + got[2 * p + i].astype(F)) * scale for i in range(2)]
        pull_high, pull_low = halves(jnp.concatenate(pulled, 1))
        grad = product(jnp.concatenate([pull_high, pull_low], 0), turned, ((0,), (0,)))
        grad_high, grad_low = halves(grad * (sig + act * (1.0 - sig)))
        in_term = product(nodes, grad_high, ((0,), (0,))) + product(nodes, grad_low, ((0,), (0,)))
        out_term = product(pull_high, high) + product(pull_high, low) + product(pull_low, high)
        return in_term, out_term

    def body(step, carry):
        terms = [two_tiles(step * DENSE_UNROLL + u) for u in range(DENSE_UNROLL)]
        in_sum[...] += sum(term[0] for term in terms)
        out_sum[...] += sum(term[1] for term in terms)
        return carry

    lax.fori_loop(0, Z // 2 // DENSE_UNROLL, body, 0)
    out_term = out_sum[...].T
    first = core[0] == 0
    for c in range(G):
        in_part = jnp.concatenate(
            [in_sum[8 * c : 8 * c + 8, T * b : T * b + T] for b in range(4)], 0
        )
        out_part = out_term[S * c : S * c + S]
        own[c] = jnp.where(first, in_part, out_part)
        other[c] = jnp.where(first, out_part, in_part)


def merge(own, got, out):
    out[:, 0:S], out[:, S:] = halves(own[...] + got[...])


def share(terms, unused_high, unused_low, out):
    total = jnp.zeros((S, T), F)
    for c in range(G):
        total = total + (terms[c, 0:S].astype(F) + terms[c, S:].astype(F))
    for z in range(Z):
        out[z] = total


def finish(slices, second, logits, in_grad, out_grad):
    total = second[0, 0:T].astype(F)
    for c in range(1, G):
        total = total + second[c, 0:T].astype(F)
    logits[...] = total
    for c in range(G):
        piece = slices[0, c].astype(F)
        for b in range(4):
            in_grad[8 * c : 8 * c + 8, T * b : T * b + T] = piece[8 * b : 8 * b + 8]
        out_grad[S * c : S * c + S] = slices[1, c].astype(F)


SAME_CORE = [[2 * z + core for z in range(Z)] for core in range(2)]
SAME_CHIP = [[2 * z, 2 * z + 1] for z in range(Z)]


def swap(value, axis, groups=None):
    return lax.all_to_all(value, axis, 0, 0, tiled=True, axis_index_groups=groups)


def to_all(value, count):
    return jnp.broadcast_to(value[None], (count,) + value.shape)


def both_cores(value):
    return lax.all_gather(value, "row", axis=0, axis_index_groups=SAME_CHIP)


def other_core(value):
    return lax.ppermute(value, "row", [(i, i ^ 1) for i in range(G)])


def on_device(node_input, adj_tiles, tile_row, tile_col, weight_in, weight_out, logit_grad):
    tiles = adj_tiles.reshape(-1, T, T)
    rows = tile_row.reshape(-1)
    cols = tile_col.reshape(-1)
    core = (lax.axis_index("row") % 2).reshape(1)
    scale = 1.0 / math.sqrt(node_input.shape[0] * G * G)
    spread_flops = 2 * tiles.shape[0] * T**3
    width = weight_in.shape[1]
    sds = jax.ShapeDtypeStruct
    steps = tiles.shape[0] // UNROLL
    blocks = (G, T, T)
    stream = [
        pltpu.VMEM(tiles.shape, B),
        pltpu.SemaphoreType.DMA((steps,)),
        pltpu.SMEM((2, tiles.shape[0]), jnp.int32),
        pltpu.SemaphoreType.DMA((3,)),
    ]
    rows, cols, tiles, grads = (
        pltpu.with_memory_space_constraint(array, pltpu.HBM)
        for array in (rows, cols, tiles, logit_grad)
    )

    x_all = lax.all_gather(node_input, "row", axis=0)
    first = kernel_call(
        spread_first, "spread_first", spread_flops, sds((G, 2 * T, T), B),
        [ANY, ANY, ANY, VMEM, ANY], stream + [pltpu.VMEM((T, T), B), pltpu.VMEM(blocks, F)],
    )(rows, cols, tiles, x_all, grads)
    received = swap(first, "col")
    agg = kernel_call(collect, "collect", 0, sds((Z, T, T), B), [VMEM])(received)
    agg = swap(agg, "row", SAME_CORE)
    keep, send = kernel_call(
        spread_back, "spread_back", spread_flops, (sds((Z, T, T), F), sds((Z, T, T), B)),
        [SMEM, ANY, ANY, ANY, VMEM], stream + [pltpu.VMEM(blocks, B), pltpu.VMEM(blocks, F)],
    )(core, rows, cols, tiles, received)
    got = other_core(send)

    *proj, own, other = kernel_call(
        functools.partial(dense, scale), "dense", 20 * Z * T * T * width,
        (sds((Z, T, T), B), sds((Z, T, T), B), sds((G, S, T), F), sds((G, S, T), F)),
        [SMEM] + [VMEM] * 5,
        [pltpu.VMEM((T, width), F), pltpu.VMEM((T, width), F)],
    )(core, agg.reshape(Z // 2, 2 * T, T), keep, got, weight_in, weight_out)
    terms = kernel_call(merge, "merge", 0, sds((G, 2 * S, T), B), [VMEM, VMEM])(
        own, other_core(other)
    )
    terms = swap(terms, "col")
    proj = [both_cores(part) for part in proj]
    col_sum = kernel_call(share, "share", 0, sds((Z, S, T), F), [VMEM, ANY, ANY])(terms, *proj)
    second = kernel_call(
        spread_second, "spread_second", spread_flops, sds((G, T + S, T), B),
        [ANY, ANY, ANY, VMEM, VMEM], stream + [pltpu.VMEM(blocks, F)],
    )(rows, cols, tiles, *proj)

    total = swap(col_sum, "row", SAME_CORE).sum(0).astype(B)
    second = second.at[:, T:].set(to_all(total, G))
    second = swap(second, "col")
    return kernel_call(
        finish, "finish", 0, (sds((T, T), F), sds((T, width), F), sds((width, T), F)),
        [VMEM, VMEM],
    )(both_cores(second[:, T:]), second)


def solution(mesh):
    placed = (
        P(("row", "col"), None),
        P("row", "col", None, None, None),
        P("row", "col", None),
        P("row", "col", None),
        P(),
        P(),
        P(("row", "col"), None),
    )
    return jax.shard_map(
        on_device,
        mesh=mesh,
        in_specs=placed,
        out_specs=(P(("row", "col"), None), P(), P()),
        check_vma=False,
    )
```

time: 795 us -> 116 us (0.15)
  waiting for transfers between devices: 424 us -> 12.9 us
  other arithmetic: 160 us -> 0.01 us
  matrix products: 89.7 us -> 0 us
  local copies, waits for them, and re-layouts: 71.7 us -> 0.06 us
  blocking collectives: 24.4 us -> 68.8 us
  Pallas kernels: 0 us -> 17.3 us
  starting transfers between devices: 0.43 us -> 16 us
  between operations: 14.2 us -> 0.73 us
  loops' own time: 7.95 us -> 0 us
    psum x1 -> x0, waiting for transfers between devices: 255 us -> none  [on_device(): w_in_grad, w_out_grad = lax.psum((in_term, out_term), ('row', 'col'))]
    scatter-add x12 -> x0, other arithmetic: 157 us -> none  [add_block(): return (totals.at[target].add(product), None)]
    reduce_scatter x3 -> x0, waiting for transfers between devices: 129 us -> none  [the longest x1 74 us: on_device(): lax.psum_scatter(partial_in, 'col', scatter_dimension=0, tiled=True)]
    dot_general x17 -> x0, matrix products: 89.7 us -> none  [the longest x4 44.8 us: add_block(): jnp.einsum(pattern, chosen.astype(jnp.float32), picked, precision=lax.Pre...]
    gather x12 -> x0, local copies, waits for them, and re-layouts: 48.1 us -> none  [add_block(): picked = blocks[source]]
    all_gather x2 -> x0, waiting for transfers between devices: 40.4 us -> none  [the longest x1 40.4 us: on_device(): gathered_hid = lax.all_gather(hidden, 'row', axis=0, tiled=True)]
    all_to_all x0 -> x2, blocking collectives: none -> 36.4 us  [swap(): lax.all_to_all(value, axis, 0, 0, tiled=True, axis_index_groups=groups)]
    pallas_call x0 -> x8, Pallas kernels: none -> 17.3 us  [the longest x1 4.19 us: on_device(): kernel_call(spread_second, 'spread_second', spread_flops, sds((G, T + S,...]
  transfers between devices with their start and end apart: 6 -> 5, of which waited for: 4 -> 5; matrix products, arithmetic and copies ran while one was open for 35% -> 0% of each run, Pallas kernels for 0% -> 6%
where the time goes in v2:
time: 116 us
  blocking collectives  68.8 us (59%)
  Pallas kernels  17.3 us (15%)
  starting transfers between devices  16 us (14%)
  waiting for transfers between devices  12.9 us (11%)
    all_to_all x2, blocking collectives, swap(): lax.all_to_all(value, axis, 0, 0, tiled=True, axis_index_groups=groups)  36.4 us
    all_gather x1, blocking collectives, on_device(): x_all = lax.all_gather(node_input, 'row', axis=0)  23 us
    all_to_all x3, waiting for transfers between devices, swap(): lax.all_to_all(value, axis, 0, 0, tiled=True, axis_index_groups=groups)  10.5 us
    all_to_all x3, starting transfers between devices, swap(): lax.all_to_all(value, axis, 0, 0, tiled=True, axis_index_groups=groups)  10.5 us
    all_gather x3, blocking collectives, both_cores(): return lax.all_gather(value, 'row', axis=0, axis_index_groups=SAME_CHIP)  9.39 us
    ppermute x2, starting transfers between devices, other_core(): return lax.ppermute(value, 'row', [(i, i ^ 1) for i in range(G)])  5.49 us
    pallas_call x1, Pallas kernels, on_device(): kernel_call(spread_second, 'spread_second', spread_flops, sds((G, T + S,...  4.19 us
    pallas_call x1, Pallas kernels, on_device(): kernel_call(spread_first, 'spread_first', spread_flops, sds((G, 2 * T, T)...  3.7 us
  transfers between devices with their start and end apart: 5, of which 5 were waited for; matrix products, arithmetic and copies ran while one was open for 0% of the time, Pallas kernels for 6%

profile of v2, /device:TPU:1, one launch (start us, length us, event | category | flops | bytes accessed | tf_op | source)
XLA Modules:
  0.0 115.7 jit_solution(5091936866920363441)
XLA Ops:
  0.6 23.0 %all-gather = bf16[2048,128]{1,0:T(8,128)(2,1)S(1)} all-gather(bf16[128,128]{1,0:T(8,128)(2,1)} %param.9), channel_id=2, replica_groups=mesh['row'=16,'col'=16] {'row'}, dimensions={0}, use_global_device_ids=true | all-gather | bytes 557056 | tf_op jit(solution)/shard_map/all_gather | solution.py:250
  23.6 3.7 %spread_first.1 = bf16[16,256,128]{2,1,0:T(8,128)(2,1)S(1)} custom-call(s32[128]{0:T(128)} %bitcast.19, s32[128]{0:T(128)} %bitcast.22, bf16[128,128,128]{2,1,0:T(8,128)(2,1)} %bitcast.16, bf16[16,128,128]{2,1,0:T(8,128)(2,1)S(1)} %bitcast.13, bf16[128,128]{1,0:T(8,128)(2,1)} %grads.1), custom_call_target="tpu_custom_call" | custom-call | flops 536870912 | bytes 6291456 | tf_op jit(solution)/shard_map/spread_first/pallas_call | solution.py:251
  27.4 23.2 %all_to_all.25.received = bf16[16,256,128]{2,1,0:T(8,128)(2,1)S(1)} all-to-all(bf16[16,256,128]{2,1,0:T(8,128)(2,1)S(1)} %spread_first.1), channel_id=1, replica_groups=mesh['row'=16,'col'=16] {'col'}, dimensions={0} | all-to-all | bytes 2097152 | tf_op jit(solution)/shard_map/all_to_all | solution.py:213
  50.6 0.8 collect.1
  51.4 3.4 %all-to-all-start.1 = ((bf16[8,128,128]{2,1,0:T(8,128)(2,1)}), bf16[8,128,128]{2,1,0:T(8,128)(2,1)S(1)}, u32[]{:S(2)}, u32[]{:S(2)}) async-start(bf16[8,128,128]{2,1,0:T(8,128)(2,1)} %collect.1), calls=%async_computation.1 | async-start | bytes 524288 | tf_op jit(solution)/shard_map/all_to_all | solution.py:213
  54.8 3.2 %spread_back.1 = (f32[8,128,128]{2,1,0:T(8,128)S(1)}, bf16[8,128,128]{2,1,0:T(8,128)(2,1)S(1)}) custom-call(s32[1]{0:T(128)} %bitcast.3.core, s32[128]{0:T(128)} %bitcast.20, s32[128]{0:T(128)} %bitcast.23, bf16[128,128,128]{2,1,0:T(8,128)(2,1)} %bitcast.17, bf16[16,256,128]{2,1,0:T(8,128)(2,1)S(1)} %all_to_all.25.received), custom_call_target="tpu_custom_call" | custom-call | flops 536870912 | bytes 6291456 | tf_op jit(solution)/shard_map/spread_back/pallas_call | solution.py:258
  58.0 1.8 %collective-permute-start = (bf16[8,128,128]{2,1,0:T(8,128)(2,1)S(1)}, bf16[8,128,128]{2,1,0:T(8,128)(2,1)S(1)}, u32[]{:S(2)}, u32[]{:S(2)}) collective-permute-start(bf16[8,128,128]{2,1,0:T(8,128)(2,1)S(1)} %get-tuple-element.22), channel_id=1, source_target_pairs={{0,16},{16,0},{32,48},{48,32},{64,80},{80,64},{96,112},{112,96},{1... | collective-permute-start | bytes 786440 | tf_op jit(solution)/shard_map/ppermute | solution.py:225
  59.8 1.2 %collective-permute-done.got = bf16[8,128,128]{2,1,0:T(8,128)(2,1)S(1)} collective-permute-done((bf16[8,128,128]{2,1,0:T(8,128)(2,1)S(1)}, bf16[8,128,128]{2,1,0:T(8,128)(2,1)S(1)}, u32[]{:S(2)}, u32[]{:S(2)}) %collective-permute-start) | collective-permute-done | bytes 262176 | tf_op jit(solution)/shard_map/ppermute | solution.py:225
  61.0 3.0 %all-to-all-done.1 = bf16[8,128,128]{2,1,0:T(8,128)(2,1)S(1)} async-done(((bf16[8,128,128]{2,1,0:T(8,128)(2,1)}), bf16[8,128,128]{2,1,0:T(8,128)(2,1)S(1)}, u32[]{:S(2)}, u32[]{:S(2)}) %all-to-all-start.1) | async-done | bytes 262176 | tf_op jit(solution)/shard_map/all_to_all | solution.py:213
  64.0 3.2 %dense.1 = (bf16[8,128,128]{2,1,0:T(8,128)(2,1)S(1)}, bf16[8,128,128]{2,1,0:T(8,128)(2,1)S(1)}, f32[16,32,128]{2,1,0:T(8,128)S(1)}, f32[16,32,128]{2,1,0:T(8,128)S(1)}) custom-call(s32[1]{0:T(128)} %bitcast.3.core, bf16[4,256,128]{2,1,0:T(8,128)(2,1)S(1)} %bitcast.15, f32[8,128,128]{2,1,0:T(8,128)S(1)} %get-tuple-element.21.keep, ...), custom_call_target="tpu_custom_call" | custom-call | flops 1342177280 | bytes 6291456 | tf_op jit(solution)/shard_map/dense/pallas_call | solution.py:264
  67.2 3.6 %collective-permute-start.1 = (f32[16,32,128]{2,1,0:T(8,128)S(1)}, f32[16,32,128]{2,1,0:T(8,128)S(1)}, u32[]{:S(2)}, u32[]{:S(2)}) collective-permute-start(f32[16,32,128]{2,1,0:T(8,128)S(1)} %get-tuple-element.26), channel_id=1, source_target_pairs={{0,16},{16,0},{32,48},{48,32},{64,80},{80,64},{96,112},{112,96},{1... | collective-permute-start | bytes 786440 | tf_op jit(solution)/shard_map/ppermute | solution.py:225
  70.8 1.2 %collective-permute-done.1.got = f32[16,32,128]{2,1,0:T(8,128)S(1)} collective-permute-done((f32[16,32,128]{2,1,0:T(8,128)S(1)}, f32[16,32,128]{2,1,0:T(8,128)S(1)}, u32[]{:S(2)}, u32[]{:S(2)}) %collective-permute-start.1) | collective-permute-done | bytes 262176 | tf_op jit(solution)/shard_map/ppermute | solution.py:225
  72.0 0.7 merge.1
  72.7 3.5 %all-to-all-start.2 = ((bf16[16,64,128]{2,1,0:T(8,128)(2,1)}), bf16[16,64,128]{2,1,0:T(8,128)(2,1)S(1)}, u32[]{:S(2)}, u32[]{:S(2)}) async-start(bf16[16,64,128]{2,1,0:T(8,128)(2,1)} %merge.1), calls=%async_computation.2 | async-start | bytes 524288 | tf_op jit(solution)/shard_map/all_to_all | solution.py:213
  76.2 2.2 %all-gather.1 = bf16[16,128,128]{2,1,0:T(8,128)(2,1)S(1)} all-gather(bf16[8,128,128]{2,1,0:T(8,128)(2,1)S(1)} %get-tuple-element.23), channel_id=3, replica_groups={{0,16},{32,48},{64,80},{96,112},{128,144},{160,176},{192,208},{224,240}..., dimensions={0}, use_global_device_ids=true | all-gather | bytes 786432 | tf_op jit(solution)/shard_map/all_gather | solution.py:221
  78.4 2.2 %all-gather.2 = bf16[16,128,128]{2,1,0:T(8,128)(2,1)S(1)} all-gather(bf16[8,128,128]{2,1,0:T(8,128)(2,1)S(1)} %get-tuple-element.24), channel_id=4, replica_groups={{0,16},{32,48},{64,80},{96,112},{128,144},{160,176},{192,208},{224,240}..., dimensions={0}, use_global_device_ids=true | all-gather | bytes 786432 | tf_op jit(solution)/shard_map/all_gather | solution.py:221
  80.6 4.0 %all-to-all-done.2.terms = bf16[16,64,128]{2,1,0:T(8,128)(2,1)S(1)} async-done(((bf16[16,64,128]{2,1,0:T(8,128)(2,1)}), bf16[16,64,128]{2,1,0:T(8,128)(2,1)S(1)}, u32[]{:S(2)}, u32[]{:S(2)}) %all-to-all-start.2) | async-done | bytes 262176 | tf_op jit(solution)/shard_map/all_to_all | solution.py:213
  84.6 0.7 share.1
  85.3 3.6 %all-to-all-start.3 = ((f32[8,32,128]{2,1,0:T(8,128)}), f32[8,32,128]{2,1,0:T(8,128)S(1)}, u32[]{:S(2)}, u32[]{:S(2)}) async-start(f32[8,32,128]{2,1,0:T(8,128)} %share.1), calls=%async_computation.3 | async-start | bytes 262144 | tf_op jit(solution)/shard_map/all_to_all | solution.py:213
  88.8 4.2 %spread_second.1 = bf16[16,160,128]{2,1,0:T(8,128)(2,1)S(1)} custom-call(s32[128]{0:T(128)} %bitcast.21, s32[128]{0:T(128)} %bitcast.24, bf16[128,128,128]{2,1,0:T(8,128)(2,1)} %bitcast.18, bf16[2,8,128,128]{3,2,1,0:T(8,128)(2,1)S(1)} %bitcast.10, bf16[2,8,128,128]{3,2,1,0:T(8,128)(2,1)S(1)} %bitcast.12), custom_call_target="tpu_custom_call" | custom-call | flops 536870912 | bytes 6291456 | tf_op jit(solution)/shard_map/spread_second/pallas_call | solution.py:276
  93.0 3.6 %all-to-all-done.3 = f32[8,32,128]{2,1,0:T(8,128)S(1)} async-done(((f32[8,32,128]{2,1,0:T(8,128)}), f32[8,32,128]{2,1,0:T(8,128)S(1)}, u32[]{:S(2)}, u32[]{:S(2)}) %all-to-all-start.3) | async-done | bytes 131104 | tf_op jit(solution)/shard_map/all_to_all | solution.py:213
  96.6 13.2 %all_to_all.26.second = bf16[16,160,128]{2,1,0:T(8,128)(2,1)S(1)} all-to-all(bf16[16,160,128]{2,1,0:T(8,128)(2,1)S(1)} %broadcast_dynamic-update-slice_fusion), channel_id=1, replica_groups=mesh['row'=16,'col'=16] {'col'}, dimensions={0} | all-to-all | bytes 1310720 | tf_op jit(solution)/shard_map/all_to_all | solution.py:213
  109.8 5.0 %all-gather.3 = bf16[32,32,128]{2,1,0:T(8,128)(2,1)S(1)} all-gather(bf16[16,32,128]{2,1,0:T(8,128)(2,1)S(1)} %slice.26), channel_id=5, replica_groups={{0,16},{32,48},{64,80},{96,112},{128,144},{160,176},{192,208},{224,240}..., dimensions={0}, use_global_device_ids=true | all-gather | bytes 393216 | tf_op jit(solution)/shard_map/all_gather | solution.py:221
  114.9 0.8 finish.1
  (7 shorter events, 0.1 us)
Async XLA Ops:
  27.3 36.6 %copy-start = (bf16[128,512]{1,0:T(8,128)(2,1)S(1)}, bf16[128,512]{1,0:T(8,128)(2,1)}, u32[]{:S(2)}) copy-start(bf16[128,512]{1,0:T(8,128)(2,1)} %w_in.1) | copy-start | bytes 393220
  27.4 36.6 %copy-start.1 = (bf16[512,128]{1,0:T(8,128)(2,1)S(1)}, bf16[512,128]{1,0:T(8,128)(2,1)}, u32[]{:S(2)}) copy-start(bf16[512,128]{1,0:T(8,128)(2,1)} %w_out.1) | copy-start | bytes 393220
  51.4 12.6 %all-to-all-start.1 = ((bf16[8,128,128]{2,1,0:T(8,128)(2,1)}), bf16[8,128,128]{2,1,0:T(8,128)(2,1)S(1)}, u32[]{:S(2)}, u32[]{:S(2)}) async-start(bf16[8,128,128]{2,1,0:T(8,128)(2,1)} %collect.1), calls=%async_computation.1 | async-start | bytes 524288 | tf_op jit(solution)/shard_map/all_to_all | solution.py:213
  58.0 3.0 %collective-permute-start = (bf16[8,128,128]{2,1,0:T(8,128)(2,1)S(1)}, bf16[8,128,128]{2,1,0:T(8,128)(2,1)S(1)}, u32[]{:S(2)}, u32[]{:S(2)}) collective-permute-start(bf16[8,128,128]{2,1,0:T(8,128)(2,1)S(1)} %get-tuple-element.22), channel_id=1, source_target_pairs={{0,16},{16,0},{32,48},{48,32},{64,80},{80,64},{96,112},{112,96},{1... | collective-permute-start | bytes 786440 | tf_op jit(solution)/shard_map/ppermute | solution.py:225
  67.2 4.8 %collective-permute-start.1 = (f32[16,32,128]{2,1,0:T(8,128)S(1)}, f32[16,32,128]{2,1,0:T(8,128)S(1)}, u32[]{:S(2)}, u32[]{:S(2)}) collective-permute-start(f32[16,32,128]{2,1,0:T(8,128)S(1)} %get-tuple-element.26), channel_id=1, source_target_pairs={{0,16},{16,0},{32,48},{48,32},{64,80},{80,64},{96,112},{112,96},{1... | collective-permute-start | bytes 786440 | tf_op jit(solution)/shard_map/ppermute | solution.py:225
  72.7 11.9 %all-to-all-start.2 = ((bf16[16,64,128]{2,1,0:T(8,128)(2,1)}), bf16[16,64,128]{2,1,0:T(8,128)(2,1)S(1)}, u32[]{:S(2)}, u32[]{:S(2)}) async-start(bf16[16,64,128]{2,1,0:T(8,128)(2,1)} %merge.1), calls=%async_computation.2 | async-start | bytes 524288 | tf_op jit(solution)/shard_map/all_to_all | solution.py:213
  85.3 11.3 %all-to-all-start.3 = ((f32[8,32,128]{2,1,0:T(8,128)}), f32[8,32,128]{2,1,0:T(8,128)S(1)}, u32[]{:S(2)}, u32[]{:S(2)}) async-start(f32[8,32,128]{2,1,0:T(8,128)} %share.1), calls=%async_computation.3 | async-start | bytes 262144 | tf_op jit(solution)/shard_map/all_to_all | solution.py:213

commit v3 on v2

--- a/solution.py
+++ b/solution.py
@@ -16,7 +16,7 @@
 G = 16
 Z = 8
 S = 32
-UNROLL = 32
+UNROLL = 64
 DENSE_UNROLL = 4
 
 
@@ -75,7 +75,7 @@
         out[i, T:] = own[...]
 
 
-def spread_second(rows, cols, tiles, high, low, out, held, sems, ids, more, total):
+def spread_second(rows, cols, tiles, feats, out, held, sems, ids, more, total):
     copies = fetch([(rows, ids.at[0]), (cols, ids.at[1])], more)
 
     def before():
@@ -84,9 +84,7 @@
 
     def product(tile, k):
         q = ids[1, k]
-        twice = jnp.concatenate([tile, tile], 1)
-        feats = jnp.concatenate([part[q & 1, q >> 1] for part in (high, low)], 0)
-        return jnp.dot(twice, feats, preferred_element_type=F)
+        return jnp.dot(tile, feats[q & 1, q >> 1], preferred_element_type=F)
 
     each_tile(tiles, held, sems, total, before, product, lambda k: ids[0, k])
     for i in range(G):
@@ -139,7 +137,7 @@
 
 
 def dense(scale, core, agg, keep, got, w_in, w_out, *refs):
-    *proj, own, other, in_sum, out_sum = refs
+    proj, own, other, in_sum, out_sum = refs
     in_sum[...] = jnp.zeros_like(in_sum)
     out_sum[...] = jnp.zeros_like(out_sum)
     turned = w_out[...].T
@@ -151,10 +149,9 @@
         sig = jax.nn.sigmoid(pre)
         act = pre * sig
         high, low = halves(act)
-        projected = halves(product(high, w_out[...]) + product(low, w_out[...]))
+        projected = (product(high, w_out[...]) + product(low, w_out[...])).astype(B)
         for i in range(2):
-            for part in range(2):
-                proj[part][2 * p + i] = projected[part][i * T : i * T + T]
+            proj[2 * p + i] = projected[i * T : i * T + T]
         pulled = [(keep[2 * p + i] + got[2 * p + i].astype(F)) * scale for i in range(2)]
         pull_high, pull_low = halves(jnp.concatenate(pulled, 1))
         grad = product(jnp.concatenate([pull_high, pull_low], 0), turned, ((0,), (0,)))
@@ -185,7 +182,7 @@
     out[:, 0:S], out[:, S:] = halves(own[...] + got[...])
 
 
-def share(terms, unused_high, unused_low, out):
+def share(terms, out):
     total = jnp.zeros((S, T), F)
     for c in range(G):
         total = total + (terms[c, 0:S].astype(F) + terms[c, S:].astype(F))
@@ -261,9 +258,9 @@
     )(core, rows, cols, tiles, received)
     got = other_core(send)
 
-    *proj, own, other = kernel_call(
+    proj, own, other = kernel_call(
         functools.partial(dense, scale), "dense", 20 * Z * T * T * width,
-        (sds((Z, T, T), B), sds((Z, T, T), B), sds((G, S, T), F), sds((G, S, T), F)),
+        (sds((Z, T, T), B), sds((G, S, T), F), sds((G, S, T), F)),
         [SMEM] + [VMEM] * 5,
         [pltpu.VMEM((T, width), F), pltpu.VMEM((T, width), F)],
     )(core, agg.reshape(Z // 2, 2 * T, T), keep, got, weight_in, weight_out)
@@ -271,12 +268,12 @@
         own, other_core(other)
     )
     terms = swap(terms, "col")
-    proj = [both_cores(part) for part in proj]
-    col_sum = kernel_call(share, "share", 0, sds((Z, S, T), F), [VMEM, ANY, ANY])(terms, *proj)
+    proj = both_cores(proj)
+    col_sum = kernel_call(share, "share", 0, sds((Z, S, T), F), [VMEM])(terms)
     second = kernel_call(
         spread_second, "spread_second", spread_flops, sds((G, T + S, T), B),
-        [ANY, ANY, ANY, VMEM, VMEM], stream + [pltpu.VMEM(blocks, F)],
-    )(rows, cols, tiles, *proj)
+        [ANY, ANY, ANY, VMEM], stream + [pltpu.VMEM(blocks, F)],
+    )(rows, cols, tiles, proj)
 
     total = swap(col_sum, "row", SAME_CORE).sum(0).astype(B)
     second = second.at[:, T:].set(to_all(total, G))

time: 116 us -> 114 us (0.983)
  blocking collectives: 68.8 us -> 78.9 us
  waiting for transfers between devices: 12.9 us -> 6.65 us
  starting transfers between devices: 16 us -> 12 us
  Pallas kernels: 17.3 us -> 15.5 us
    all_to_all x2 -> x3, blocking collectives: 36.4 us -> 47.2 us  [swap(): lax.all_to_all(value, axis, 0, 0, tiled=True, axis_index_groups=groups)]
    all_to_all x3 -> x2, waiting for transfers between devices: 10.5 us -> 4.32 us  [swap(): lax.all_to_all(value, axis, 0, 0, tiled=True, axis_index_groups=groups)]
    all_to_all x3 -> x2, starting transfers between devices: 10.5 us -> 6.78 us  [swap(): lax.all_to_all(value, axis, 0, 0, tiled=True, axis_index_groups=groups)]
    all_gather x3 -> x2, blocking collectives: 9.39 us -> 8.7 us  [both_cores(): return lax.all_gather(value, 'row', axis=0, axis_index_groups=SAME_CHIP)]
  transfers between devices with their start and end apart: 5 -> 4, of which waited for: 5 -> 4; matrix products, arithmetic and copies ran while one was open for 0% -> 0% of each run, Pallas kernels for 6% -> 6%
where the time goes in v3:
time: 114 us
  blocking collectives  78.9 us (69%)
  Pallas kernels  15.5 us (14%)
  starting transfers between devices  12 us (11%)
  waiting for transfers between devices  6.65 us (6%)
    all_to_all x3, blocking collectives, swap(): lax.all_to_all(value, axis, 0, 0, tiled=True, axis_index_groups=groups)  47.2 us
    all_gather x1, blocking collectives, on_device(): x_all = lax.all_gather(node_input, 'row', axis=0)  23 us
    all_gather x2, blocking collectives, both_cores(): return lax.all_gather(value, 'row', axis=0, axis_index_groups=SAME_CHIP)  8.7 us
    all_to_all x2, starting transfers between devices, swap(): lax.all_to_all(value, axis, 0, 0, tiled=True, axis_index_groups=groups)  6.78 us
    ppermute x2, starting transfers between devices, other_core(): return lax.ppermute(value, 'row', [(i, i ^ 1) for i in range(G)])  5.24 us
    all_to_all x2, waiting for transfers between devices, swap(): lax.all_to_all(value, axis, 0, 0, tiled=True, axis_index_groups=groups)  4.32 us
    pallas_call x1, Pallas kernels, on_device(): kernel_call(spread_second, 'spread_second', spread_flops, sds((G, T + S,...  3.34 us
    pallas_call x1, Pallas kernels, on_device(): kernel_call(spread_first, 'spread_first', spread_flops, sds((G, 2 * T, T)...  3.32 us
  transfers between devices with their start and end apart: 4, of which 4 were waited for; matrix products, arithmetic and copies ran while one was open for 0% of the time, Pallas kernels for 6%

profile of v3, /device:TPU:1, one launch (start us, length us, event | category | flops | bytes accessed | tf_op | source)
XLA Modules:
  0.0 113.8 jit_solution(8944831578354865731)
XLA Ops:
  0.6 23.0 %all-gather = bf16[2048,128]{1,0:T(8,128)(2,1)S(1)} all-gather(bf16[128,128]{1,0:T(8,128)(2,1)} %param.9), channel_id=2, replica_groups=mesh['row'=16,'col'=16] {'row'}, dimensions={0}, use_global_device_ids=true | all-gather | bytes 557056 | tf_op jit(solution)/shard_map/all_gather | solution.py:247
  23.6 3.3 %spread_first.1 = bf16[16,256,128]{2,1,0:T(8,128)(2,1)S(1)} custom-call(s32[128]{0:T(128)} %bitcast.15, s32[128]{0:T(128)} %bitcast.18, bf16[128,128,128]{2,1,0:T(8,128)(2,1)} %bitcast.12, bf16[16,128,128]{2,1,0:T(8,128)(2,1)S(1)} %bitcast.9, bf16[128,128]{1,0:T(8,128)(2,1)} %grads.1), custom_call_target="tpu_custom_call" | custom-call | flops 536870912 | bytes 6291456 | tf_op jit(solution)/shard_map/spread_first/pallas_call | solution.py:248
  27.0 0.0 copy-start
  27.0 0.0 copy-start.1
  27.0 23.3 %all_to_all.25.received = bf16[16,256,128]{2,1,0:T(8,128)(2,1)S(1)} all-to-all(bf16[16,256,128]{2,1,0:T(8,128)(2,1)S(1)} %spread_first.1), channel_id=1, replica_groups=mesh['row'=16,'col'=16] {'col'}, dimensions={0} | all-to-all | bytes 2097152 | tf_op jit(solution)/shard_map/all_to_all | solution.py:210
  50.3 0.8 collect.1
  51.0 3.4 %all-to-all-start.1 = ((bf16[8,128,128]{2,1,0:T(8,128)(2,1)}), bf16[8,128,128]{2,1,0:T(8,128)(2,1)S(1)}, u32[]{:S(2)}, u32[]{:S(2)}) async-start(bf16[8,128,128]{2,1,0:T(8,128)(2,1)} %collect.1), calls=%async_computation.1 | async-start | bytes 524288 | tf_op jit(solution)/shard_map/all_to_all | solution.py:210
  54.5 3.2 %spread_back.1 = (f32[8,128,128]{2,1,0:T(8,128)S(1)}, bf16[8,128,128]{2,1,0:T(8,128)(2,1)S(1)}) custom-call(s32[1]{0:T(128)} %bitcast.3.core, s32[128]{0:T(128)} %bitcast.16, s32[128]{0:T(128)} %bitcast.19, bf16[128,128,128]{2,1,0:T(8,128)(2,1)} %bitcast.13, bf16[16,256,128]{2,1,0:T(8,128)(2,1)S(1)} %all_to_all.25.received), custom_call_target="tpu_custom_call" | custom-call | flops 536870912 | bytes 6291456 | tf_op jit(solution)/shard_map/spread_back/pallas_call | solution.py:255
  57.7 1.8 %collective-permute-start = (bf16[8,128,128]{2,1,0:T(8,128)(2,1)S(1)}, bf16[8,128,128]{2,1,0:T(8,128)(2,1)S(1)}, u32[]{:S(2)}, u32[]{:S(2)}) collective-permute-start(bf16[8,128,128]{2,1,0:T(8,128)(2,1)S(1)} %get-tuple-element.21), channel_id=1, source_target_pairs={{0,16},{16,0},{32,48},{48,32},{64,80},{80,64},{96,112},{112,96},{1... | collective-permute-start | bytes 786440 | tf_op jit(solution)/shard_map/ppermute | solution.py:222
  59.5 1.2 %collective-permute-done.got = bf16[8,128,128]{2,1,0:T(8,128)(2,1)S(1)} collective-permute-done((bf16[8,128,128]{2,1,0:T(8,128)(2,1)S(1)}, bf16[8,128,128]{2,1,0:T(8,128)(2,1)S(1)}, u32[]{:S(2)}, u32[]{:S(2)}) %collective-permute-start) | collective-permute-done | bytes 262176 | tf_op jit(solution)/shard_map/ppermute | solution.py:222
  60.7 3.1 %all-to-all-done.1 = bf16[8,128,128]{2,1,0:T(8,128)(2,1)S(1)} async-done(((bf16[8,128,128]{2,1,0:T(8,128)(2,1)}), bf16[8,128,128]{2,1,0:T(8,128)(2,1)S(1)}, u32[]{:S(2)}, u32[]{:S(2)}) %all-to-all-start.1) | async-done | bytes 262176 | tf_op jit(solution)/shard_map/all_to_all | solution.py:210
  63.8 0.0 copy-done
  63.9 3.2 %dense.1 = (bf16[8,128,128]{2,1,0:T(8,128)(2,1)S(1)}, f32[16,32,128]{2,1,0:T(8,128)S(1)}, f32[16,32,128]{2,1,0:T(8,128)S(1)}) custom-call(s32[1]{0:T(128)} %bitcast.3.core, bf16[4,256,128]{2,1,0:T(8,128)(2,1)S(1)} %bitcast.11, f32[8,128,128]{2,1,0:T(8,128)S(1)} %get-tuple-element.20.keep, bf16[8,128,128]{2,1,0:T(8,128)(2,1)S(1)} %collective-permute-done.got, ...), custom_call_target="tpu_custom_call" | custom-call | flops 1342177280 | bytes 6291456 | tf_op jit(solution)/shard_map/dense/pallas_call | solution.py:261
  67.0 3.4 %collective-permute-start.1 = (f32[16,32,128]{2,1,0:T(8,128)S(1)}, f32[16,32,128]{2,1,0:T(8,128)S(1)}, u32[]{:S(2)}, u32[]{:S(2)}) collective-permute-start(f32[16,32,128]{2,1,0:T(8,128)S(1)} %get-tuple-element.24), channel_id=1, source_target_pairs={{0,16},{16,0},{32,48},{48,32},{64,80},{80,64},{96,112},{112,96},{1... | collective-permute-start | bytes 786440 | tf_op jit(solution)/shard_map/ppermute | solution.py:222
  70.5 1.2 %collective-permute-done.1.got = f32[16,32,128]{2,1,0:T(8,128)S(1)} collective-permute-done((f32[16,32,128]{2,1,0:T(8,128)S(1)}, f32[16,32,128]{2,1,0:T(8,128)S(1)}, u32[]{:S(2)}, u32[]{:S(2)}) %collective-permute-start.1) | collective-permute-done | bytes 262176 | tf_op jit(solution)/shard_map/ppermute | solution.py:222
  71.7 11.2 %all_to_all.26.terms = bf16[16,64,128]{2,1,0:T(8,128)(2,1)S(1)} all-to-all(bf16[16,64,128]{2,1,0:T(8,128)(2,1)S(1)} %merge.1), channel_id=1, replica_groups=mesh['row'=16,'col'=16] {'col'}, dimensions={0} | all-to-all | bytes 524288 | tf_op jit(solution)/shard_map/all_to_all | solution.py:210
  82.8 0.7 share.1
  83.5 3.4 %all-to-all-start.3 = ((f32[8,32,128]{2,1,0:T(8,128)}), f32[8,32,128]{2,1,0:T(8,128)S(1)}, u32[]{:S(2)}, u32[]{:S(2)}) async-start(f32[8,32,128]{2,1,0:T(8,128)} %share.1), calls=%async_computation.3 | async-start | bytes 262144 | tf_op jit(solution)/shard_map/all_to_all | solution.py:210
  86.9 3.3 %all-gather.1 = bf16[16,128,128]{2,1,0:T(8,128)(2,1)S(1)} all-gather(bf16[8,128,128]{2,1,0:T(8,128)(2,1)S(1)} %get-tuple-element.22), channel_id=3, replica_groups={{0,16},{32,48},{64,80},{96,112},{128,144},{160,176},{192,208},{224,240}..., dimensions={0}, use_global_device_ids=true | all-gather | bytes 786432 | tf_op jit(solution)/shard_map/all_gather | solution.py:218
  90.2 3.3 %spread_second.1 = bf16[16,160,128]{2,1,0:T(8,128)(2,1)S(1)} custom-call(s32[128]{0:T(128)} %bitcast.17, s32[128]{0:T(128)} %bitcast.20, bf16[128,128,128]{2,1,0:T(8,128)(2,1)} %bitcast.14, bf16[2,8,128,128]{3,2,1,0:T(8,128)(2,1)S(1)} %bitcast.8), custom_call_target="tpu_custom_call" | custom-call | flops 536870912 | bytes 6291456 | tf_op jit(solution)/shard_map/spread_second/pallas_call | solution.py:273
  93.6 1.2 %all-to-all-done.3 = f32[8,32,128]{2,1,0:T(8,128)S(1)} async-done(((f32[8,32,128]{2,1,0:T(8,128)}), f32[8,32,128]{2,1,0:T(8,128)S(1)}, u32[]{:S(2)}, u32[]{:S(2)}) %all-to-all-start.3) | async-done | bytes 131104 | tf_op jit(solution)/shard_map/all_to_all | solution.py:210
  94.8 12.8 %all_to_all.27.second = bf16[16,160,128]{2,1,0:T(8,128)(2,1)S(1)} all-to-all(bf16[16,160,128]{2,1,0:T(8,128)(2,1)S(1)} %broadcast_dynamic-update-slice_fusion), channel_id=1, replica_groups=mesh['row'=16,'col'=16] {'col'}, dimensions={0} | all-to-all | bytes 1310720 | tf_op jit(solution)/shard_map/all_to_all | solution.py:210
  107.6 5.4 %all-gather.2 = bf16[32,32,128]{2,1,0:T(8,128)(2,1)S(1)} all-gather(bf16[16,32,128]{2,1,0:T(8,128)(2,1)S(1)} %slice.26), channel_id=4, replica_groups={{0,16},{32,48},{64,80},{96,112},{128,144},{160,176},{192,208},{224,240}..., dimensions={0}, use_global_device_ids=true | all-gather | bytes 393216 | tf_op jit(solution)/shard_map/all_gather | solution.py:218
  112.9 0.8 finish.1
  (5 shorter events, 0.1 us)
Async XLA Ops:
  27.0 36.9 %copy-start = (bf16[128,512]{1,0:T(8,128)(2,1)S(1)}, bf16[128,512]{1,0:T(8,128)(2,1)}, u32[]{:S(2)}) copy-start(bf16[128,512]{1,0:T(8,128)(2,1)} %w_in.1) | copy-start | bytes 393220
  27.0 36.9 %copy-start.1 = (bf16[512,128]{1,0:T(8,128)(2,1)S(1)}, bf16[512,128]{1,0:T(8,128)(2,1)}, u32[]{:S(2)}) copy-start(bf16[512,128]{1,0:T(8,128)(2,1)} %w_out.1) | copy-start | bytes 393220
  51.0 12.8 %all-to-all-start.1 = ((bf16[8,128,128]{2,1,0:T(8,128)(2,1)}), bf16[8,128,128]{2,1,0:T(8,128)(2,1)S(1)}, u32[]{:S(2)}, u32[]{:S(2)}) async-start(bf16[8,128,128]{2,1,0:T(8,128)(2,1)} %collect.1), calls=%async_computation.1 | async-start | bytes 524288 | tf_op jit(solution)/shard_map/all_to_all | solution.py:210
  57.7 3.0 %collective-permute-start = (bf16[8,128,128]{2,1,0:T(8,128)(2,1)S(1)}, bf16[8,128,128]{2,1,0:T(8,128)(2,1)S(1)}, u32[]{:S(2)}, u32[]{:S(2)}) collective-permute-start(bf16[8,128,128]{2,1,0:T(8,128)(2,1)S(1)} %get-tuple-element.21), channel_id=1, source_target_pairs={{0,16},{16,0},{32,48},{48,32},{64,80},{80,64},{96,112},{112,96},{1... | collective-permute-start | bytes 786440 | tf_op jit(solution)/shard_map/ppermute | solution.py:222
  67.0 4.6 %collective-permute-start.1 = (f32[16,32,128]{2,1,0:T(8,128)S(1)}, f32[16,32,128]{2,1,0:T(8,128)S(1)}, u32[]{:S(2)}, u32[]{:S(2)}) collective-permute-start(f32[16,32,128]{2,1,0:T(8,128)S(1)} %get-tuple-element.24), channel_id=1, source_target_pairs={{0,16},{16,0},{32,48},{48,32},{64,80},{80,64},{96,112},{112,96},{1... | collective-permute-start | bytes 786440 | tf_op jit(solution)/shard_map/ppermute | solution.py:222
  83.5 11.2 %all-to-all-start.3 = ((f32[8,32,128]{2,1,0:T(8,128)}), f32[8,32,128]{2,1,0:T(8,128)S(1)}, u32[]{:S(2)}, u32[]{:S(2)}) async-start(f32[8,32,128]{2,1,0:T(8,128)} %share.1), calls=%async_computation.3 | async-start | bytes 262144 | tf_op jit(solution)/shard_map/all_to_all | solution.py:210

commit v4 on v3

--- a/solution.py
+++ b/solution.py
@@ -31,6 +31,10 @@
         compiler_params=pltpu.CompilerParams(vmem_limit_bytes=limit << 20),
         name=name,
     )
+
+
+def chip_place(q):
+    return ((q >> 1) & 3) * 2 + (q >> 3)
 
 
 def fetch(pairs, sems):
@@ -84,7 +88,7 @@
 
     def product(tile, k):
         q = ids[1, k]
-        return jnp.dot(tile, feats[q & 1, q >> 1], preferred_element_type=F)
+        return jnp.dot(tile, feats[q & 1, chip_place(q)], preferred_element_type=F)
 
     each_tile(tiles, held, sems, total, before, product, lambda k: ids[0, k])
     for i in range(G):
@@ -103,7 +107,7 @@
 
     def target(k):
         q = ids[1, k]
-        return ((q & 1) ^ core[0]) * Z + (q >> 1)
+        return ((q & 1) ^ core[0]) * Z + chip_place(q)
 
     each_tile(
         tiles,
@@ -202,7 +206,7 @@
         out_grad[S * c : S * c + S] = slices[1, c].astype(F)
 
 
-SAME_CORE = [[2 * z + core for z in range(Z)] for core in range(2)]
+SAME_CORE = [[2 * z + core for z in (0, 4, 1, 5, 2, 6, 3, 7)] for core in range(2)]
 SAME_CHIP = [[2 * z, 2 * z + 1] for z in range(Z)]
 
 

time: 114 us -> 112 us (0.982)
  waiting for transfers between devices: 6.65 us -> 3.16 us
    all_to_all x2, waiting for transfers between devices: 4.32 us -> 0.84 us  [swap(): lax.all_to_all(value, axis, 0, 0, tiled=True, axis_index_groups=groups)]
  transfers between devices with their start and end apart: 4 -> 4, of which waited for: 4 -> 3; matrix products, arithmetic and copies ran while one was open for 0% -> 0% of each run, Pallas kernels for 6% -> 6%
where the time goes in v4:
time: 112 us; the launch traced here: 111 us
  blocking collectives  79.2 us (71%)
  Pallas kernels  15.4 us (14%)
  starting transfers between devices  12.6 us (11%)
  waiting for transfers between devices  3.16 us (3%)
    all_to_all x3, blocking collectives, swap(): lax.all_to_all(value, axis, 0, 0, tiled=True, axis_index_groups=groups)  47.1 us
    all_gather x1, blocking collectives, on_device(): x_all = lax.all_gather(node_input, 'row', axis=0)  23 us
    all_gather x2, blocking collectives, both_cores(): return lax.all_gather(value, 'row', axis=0, axis_index_groups=SAME_CHIP)  9.11 us
    all_to_all x2, starting transfers between devices, swap(): lax.all_to_all(value, axis, 0, 0, tiled=True, axis_index_groups=groups)  7.65 us
    ppermute x2, starting transfers between devices, other_core(): return lax.ppermute(value, 'row', [(i, i ^ 1) for i in range(G)])  4.99 us
    pallas_call x1, Pallas kernels, on_device(): kernel_call(spread_second, 'spread_second', spread_flops, sds((G, T + S,...  3.34 us
    pallas_call x1, Pallas kernels, on_device(): kernel_call(spread_first, 'spread_first', spread_flops, sds((G, 2 * T, T)...  3.32 us
    pallas_call x1, Pallas kernels, on_device(): kernel_call(spread_back, 'spread_back', spread_flops, (sds((Z, T, T), F),...  3.18 us
  transfers between devices with their start and end apart: 4, of which 3 were waited for; matrix products, arithmetic and copies ran while one was open for 0% of the time, Pallas kernels for 6%

profile of v4, /device:TPU:1, one launch (start us, length us, event | category | flops | bytes accessed | tf_op | source)
XLA Modules:
  0.0 111.1 jit_solution(116578118538696850)
XLA Ops:
  0.6 23.0 %all-gather = bf16[2048,128]{1,0:T(8,128)(2,1)S(1)} all-gather(bf16[128,128]{1,0:T(8,128)(2,1)} %param.9), channel_id=2, replica_groups=mesh['row'=16,'col'=16] {'row'}, dimensions={0}, use_global_device_ids=true | all-gather | bytes 557056 | tf_op jit(solution)/shard_map/all_gather | solution.py:251
  23.6 3.3 %spread_first.1 = bf16[16,256,128]{2,1,0:T(8,128)(2,1)S(1)} custom-call(s32[128]{0:T(128)} %bitcast.15, s32[128]{0:T(128)} %bitcast.18, bf16[128,128,128]{2,1,0:T(8,128)(2,1)} %bitcast.12, bf16[16,128,128]{2,1,0:T(8,128)(2,1)S(1)} %bitcast.9, bf16[128,128]{1,0:T(8,128)(2,1)} %grads.1), custom_call_target="tpu_custom_call" | custom-call | flops 536870912 | bytes 6291456 | tf_op jit(solution)/shard_map/spread_first/pallas_call | solution.py:252
  27.0 0.0 copy-start
  27.0 0.0 copy-start.1
  27.0 23.2 %all_to_all.25.received = bf16[16,256,128]{2,1,0:T(8,128)(2,1)S(1)} all-to-all(bf16[16,256,128]{2,1,0:T(8,128)(2,1)S(1)} %spread_first.1), channel_id=1, replica_groups=mesh['row'=16,'col'=16] {'col'}, dimensions={0} | all-to-all | bytes 2097152 | tf_op jit(solution)/shard_map/all_to_all | solution.py:214
  50.2 0.8 collect.1
  51.0 3.4 %all-to-all-start.1 = ((bf16[8,128,128]{2,1,0:T(8,128)(2,1)}), bf16[8,128,128]{2,1,0:T(8,128)(2,1)S(1)}, u32[]{:S(2)}, u32[]{:S(2)}) async-start(bf16[8,128,128]{2,1,0:T(8,128)(2,1)} %collect.1), calls=%async_computation.1 | async-start | bytes 524288 | tf_op jit(solution)/shard_map/all_to_all | solution.py:214
  54.4 3.2 %spread_back.1 = (f32[8,128,128]{2,1,0:T(8,128)S(1)}, bf16[8,128,128]{2,1,0:T(8,128)(2,1)S(1)}) custom-call(s32[1]{0:T(128)} %bitcast.3.core, s32[128]{0:T(128)} %bitcast.16, s32[128]{0:T(128)} %bitcast.19, bf16[128,128,128]{2,1,0:T(8,128)(2,1)} %bitcast.13, bf16[16,256,128]{2,1,0:T(8,128)(2,1)S(1)} %all_to_all.25.received), custom_call_target="tpu_custom_call" | custom-call | flops 536870912 | bytes 6291456 | tf_op jit(solution)/shard_map/spread_back/pallas_call | solution.py:259
  57.6 1.9 %collective-permute-start = (bf16[8,128,128]{2,1,0:T(8,128)(2,1)S(1)}, bf16[8,128,128]{2,1,0:T(8,128)(2,1)S(1)}, u32[]{:S(2)}, u32[]{:S(2)}) collective-permute-start(bf16[8,128,128]{2,1,0:T(8,128)(2,1)S(1)} %get-tuple-element.21), channel_id=1, source_target_pairs={{0,16},{16,0},{32,48},{48,32},{64,80},{80,64},{96,112},{112,96},{1... | collective-permute-start | bytes 786440 | tf_op jit(solution)/shard_map/ppermute | solution.py:226
  59.5 1.2 %collective-permute-done.got = bf16[8,128,128]{2,1,0:T(8,128)(2,1)S(1)} collective-permute-done((bf16[8,128,128]{2,1,0:T(8,128)(2,1)S(1)}, bf16[8,128,128]{2,1,0:T(8,128)(2,1)S(1)}, u32[]{:S(2)}, u32[]{:S(2)}) %collective-permute-start) | collective-permute-done | bytes 262176 | tf_op jit(solution)/shard_map/ppermute | solution.py:226
  60.6 0.8 all-to-all-done.1
  61.5 0.0 copy-done.1
  61.5 3.2 %dense.1 = (bf16[8,128,128]{2,1,0:T(8,128)(2,1)S(1)}, f32[16,32,128]{2,1,0:T(8,128)S(1)}, f32[16,32,128]{2,1,0:T(8,128)S(1)}) custom-call(s32[1]{0:T(128)} %bitcast.3.core, bf16[4,256,128]{2,1,0:T(8,128)(2,1)S(1)} %bitcast.11, f32[8,128,128]{2,1,0:T(8,128)S(1)} %get-tuple-element.20.keep, bf16[8,128,128]{2,1,0:T(8,128)(2,1)S(1)} %collective-permute-done.got, ...), custom_call_target="tpu_custom_call" | custom-call | flops 1342177280 | bytes 6291456 | tf_op jit(solution)/shard_map/dense/pallas_call | solution.py:265
  64.6 3.1 %collective-permute-start.1 = (f32[16,32,128]{2,1,0:T(8,128)S(1)}, f32[16,32,128]{2,1,0:T(8,128)S(1)}, u32[]{:S(2)}, u32[]{:S(2)}) collective-permute-start(f32[16,32,128]{2,1,0:T(8,128)S(1)} %get-tuple-element.24), channel_id=1, source_target_pairs={{0,16},{16,0},{32,48},{48,32},{64,80},{80,64},{96,112},{112,96},{1... | collective-permute-start | bytes 786440 | tf_op jit(solution)/shard_map/ppermute | solution.py:226
  67.8 1.2 %collective-permute-done.1.got = f32[16,32,128]{2,1,0:T(8,128)S(1)} collective-permute-done((f32[16,32,128]{2,1,0:T(8,128)S(1)}, f32[16,32,128]{2,1,0:T(8,128)S(1)}, u32[]{:S(2)}, u32[]{:S(2)}) %collective-permute-start.1) | collective-permute-done | bytes 262176 | tf_op jit(solution)/shard_map/ppermute | solution.py:226
  69.0 11.2 %all_to_all.26.terms = bf16[16,64,128]{2,1,0:T(8,128)(2,1)S(1)} all-to-all(bf16[16,64,128]{2,1,0:T(8,128)(2,1)S(1)} %merge.1), channel_id=1, replica_groups=mesh['row'=16,'col'=16] {'col'}, dimensions={0} | all-to-all | bytes 524288 | tf_op jit(solution)/shard_map/all_to_all | solution.py:214
  80.1 0.7 share.1
  80.8 4.2 %all-to-all-start.3 = ((f32[8,32,128]{2,1,0:T(8,128)}), f32[8,32,128]{2,1,0:T(8,128)S(1)}, u32[]{:S(2)}, u32[]{:S(2)}) async-start(f32[8,32,128]{2,1,0:T(8,128)} %share.1), calls=%async_computation.3 | async-start | bytes 262144 | tf_op jit(solution)/shard_map/all_to_all | solution.py:214
  85.1 3.6 %all-gather.1 = bf16[16,128,128]{2,1,0:T(8,128)(2,1)S(1)} all-gather(bf16[8,128,128]{2,1,0:T(8,128)(2,1)S(1)} %get-tuple-element.22), channel_id=3, replica_groups={{0,16},{32,48},{64,80},{96,112},{128,144},{160,176},{192,208},{224,240}..., dimensions={0}, use_global_device_ids=true | all-gather | bytes 786432 | tf_op jit(solution)/shard_map/all_gather | solution.py:222
  88.7 3.3 %spread_second.1 = bf16[16,160,128]{2,1,0:T(8,128)(2,1)S(1)} custom-call(s32[128]{0:T(128)} %bitcast.17, s32[128]{0:T(128)} %bitcast.20, bf16[128,128,128]{2,1,0:T(8,128)(2,1)} %bitcast.14, bf16[2,8,128,128]{3,2,1,0:T(8,128)(2,1)S(1)} %bitcast.8), custom_call_target="tpu_custom_call" | custom-call | flops 536870912 | bytes 6291456 | tf_op jit(solution)/shard_map/spread_second/pallas_call | solution.py:277
  92.0 0.0 all-to-all-done.3
  92.1 12.7 %all_to_all.27.second = bf16[16,160,128]{2,1,0:T(8,128)(2,1)S(1)} all-to-all(bf16[16,160,128]{2,1,0:T(8,128)(2,1)S(1)} %broadcast_dynamic-update-slice_fusion), channel_id=1, replica_groups=mesh['row'=16,'col'=16] {'col'}, dimensions={0} | all-to-all | bytes 1310720 | tf_op jit(solution)/shard_map/all_to_all | solution.py:214
  104.8 5.5 %all-gather.2 = bf16[32,32,128]{2,1,0:T(8,128)(2,1)S(1)} all-gather(bf16[16,32,128]{2,1,0:T(8,128)(2,1)S(1)} %slice.26), channel_id=4, replica_groups={{0,16},{32,48},{64,80},{96,112},{128,144},{160,176},{192,208},{224,240}..., dimensions={0}, use_global_device_ids=true | all-gather | bytes 393216 | tf_op jit(solution)/shard_map/all_gather | solution.py:222
  110.3 0.8 finish.1
  (5 shorter events, 0.1 us)
Async XLA Ops:
  27.0 34.5 %copy-start = (bf16[128,512]{1,0:T(8,128)(2,1)S(1)}, bf16[128,512]{1,0:T(8,128)(2,1)}, u32[]{:S(2)}) copy-start(bf16[128,512]{1,0:T(8,128)(2,1)} %w_in.1) | copy-start | bytes 393220
  27.0 34.5 %copy-start.1 = (bf16[512,128]{1,0:T(8,128)(2,1)S(1)}, bf16[512,128]{1,0:T(8,128)(2,1)}, u32[]{:S(2)}) copy-start(bf16[512,128]{1,0:T(8,128)(2,1)} %w_out.1) | copy-start | bytes 393220
  51.0 10.5 %all-to-all-start.1 = ((bf16[8,128,128]{2,1,0:T(8,128)(2,1)}), bf16[8,128,128]{2,1,0:T(8,128)(2,1)S(1)}, u32[]{:S(2)}, u32[]{:S(2)}) async-start(bf16[8,128,128]{2,1,0:T(8,128)(2,1)} %collect.1), calls=%async_computation.1 | async-start | bytes 524288 | tf_op jit(solution)/shard_map/all_to_all | solution.py:214
  57.6 3.0 %collective-permute-start = (bf16[8,128,128]{2,1,0:T(8,128)(2,1)S(1)}, bf16[8,128,128]{2,1,0:T(8,128)(2,1)S(1)}, u32[]{:S(2)}, u32[]{:S(2)}) collective-permute-start(bf16[8,128,128]{2,1,0:T(8,128)(2,1)S(1)} %get-tuple-element.21), channel_id=1, source_target_pairs={{0,16},{16,0},{32,48},{48,32},{64,80},{80,64},{96,112},{112,96},{1... | collective-permute-start | bytes 786440 | tf_op jit(solution)/shard_map/ppermute | solution.py:226
  64.6 4.3 %collective-permute-start.1 = (f32[16,32,128]{2,1,0:T(8,128)S(1)}, f32[16,32,128]{2,1,0:T(8,128)S(1)}, u32[]{:S(2)}, u32[]{:S(2)}) collective-permute-start(f32[16,32,128]{2,1,0:T(8,128)S(1)} %get-tuple-element.24), channel_id=1, source_target_pairs={{0,16},{16,0},{32,48},{48,32},{64,80},{80,64},{96,112},{112,96},{1... | collective-permute-start | bytes 786440 | tf_op jit(solution)/shard_map/ppermute | solution.py:226
  80.8 11.2 %all-to-all-start.3 = ((f32[8,32,128]{2,1,0:T(8,128)}), f32[8,32,128]{2,1,0:T(8,128)S(1)}, u32[]{:S(2)}, u32[]{:S(2)}) async-start(f32[8,32,128]{2,1,0:T(8,128)} %share.1), calls=%async_computation.3 | async-start | bytes 262144 | tf_op jit(solution)/shard_map/all_to_all | solution.py:214

commit v5 on v4

--- a/solution.py
+++ b/solution.py
@@ -34,7 +34,7 @@
 
 
 def chip_place(q):
-    return ((q >> 1) & 3) * 2 + (q >> 3)
+    return ((q >> 1) & 1) * 4 + ((q >> 1) & 2) + (q >> 3)
 
 
 def fetch(pairs, sems):
@@ -206,7 +206,7 @@
         out_grad[S * c : S * c + S] = slices[1, c].astype(F)
 
 
-SAME_CORE = [[2 * z + core for z in (0, 4, 1, 5, 2, 6, 3, 7)] for core in range(2)]
+SAME_CORE = [[2 * z + core for z in (0, 4, 2, 6, 1, 5, 3, 7)] for core in range(2)]
 SAME_CHIP = [[2 * z, 2 * z + 1] for z in range(Z)]
 
 

time: 112 us -> 112 us (level)
  no operation moved by 1% of the time
where the time goes in v5:
time: 112 us; the launch traced here: 111 us
  blocking collectives  79 us (71%)
  Pallas kernels  15.4 us (14%)
  starting transfers between devices  12.8 us (11%)
  waiting for transfers between devices  3.16 us (3%)
    all_to_all x3, blocking collectives, swap(): lax.all_to_all(value, axis, 0, 0, tiled=True, axis_index_groups=groups)  47.1 us
    all_gather x1, blocking collectives, on_device(): x_all = lax.all_gather(node_input, 'row', axis=0)  23 us
    all_gather x2, blocking collectives, both_cores(): return lax.all_gather(value, 'row', axis=0, axis_index_groups=SAME_CHIP)  8.97 us
    all_to_all x2, starting transfers between devices, swap(): lax.all_to_all(value, axis, 0, 0, tiled=True, axis_index_groups=groups)  7.59 us
    ppermute x2, starting transfers between devices, other_core(): return lax.ppermute(value, 'row', [(i, i ^ 1) for i in range(G)])  5.16 us
    pallas_call x1, Pallas kernels, on_device(): kernel_call(spread_second, 'spread_second', spread_flops, sds((G, T + S,...  3.33 us
    pallas_call x1, Pallas kernels, on_device(): kernel_call(spread_first, 'spread_first', spread_flops, sds((G, 2 * T, T)...  3.32 us
    pallas_call x1, Pallas kernels, on_device(): kernel_call(spread_back, 'spread_back', spread_flops, (sds((Z, T, T), F),...  3.18 us
  transfers between devices with their start and end apart: 4, of which 3 were waited for; matrix products, arithmetic and copies ran while one was open for 0% of the time, Pallas kernels for 6%

profile of v5, /device:TPU:1, one launch (start us, length us, event | category | flops | bytes accessed | tf_op | source)
XLA Modules:
  0.0 111.1 jit_solution(8015762045645942573)
XLA Ops:
  0.6 23.0 %all-gather = bf16[2048,128]{1,0:T(8,128)(2,1)S(1)} all-gather(bf16[128,128]{1,0:T(8,128)(2,1)} %param.9), channel_id=2, replica_groups=mesh['row'=16,'col'=16] {'row'}, dimensions={0}, use_global_device_ids=true | all-gather | bytes 557056 | tf_op jit(solution)/shard_map/all_gather | solution.py:251
  23.6 3.3 %spread_first.1 = bf16[16,256,128]{2,1,0:T(8,128)(2,1)S(1)} custom-call(s32[128]{0:T(128)} %bitcast.15, s32[128]{0:T(128)} %bitcast.18, bf16[128,128,128]{2,1,0:T(8,128)(2,1)} %bitcast.12, bf16[16,128,128]{2,1,0:T(8,128)(2,1)S(1)} %bitcast.9, bf16[128,128]{1,0:T(8,128)(2,1)} %grads.1), custom_call_target="tpu_custom_call" | custom-call | flops 536870912 | bytes 6291456 | tf_op jit(solution)/shard_map/spread_first/pallas_call | solution.py:252
  27.0 0.0 copy-start
  27.0 0.0 copy-start.1
  27.0 23.3 %all_to_all.25.received = bf16[16,256,128]{2,1,0:T(8,128)(2,1)S(1)} all-to-all(bf16[16,256,128]{2,1,0:T(8,128)(2,1)S(1)} %spread_first.1), channel_id=1, replica_groups=mesh['row'=16,'col'=16] {'col'}, dimensions={0} | all-to-all | bytes 2097152 | tf_op jit(solution)/shard_map/all_to_all | solution.py:214
  50.3 0.8 collect.1
  51.0 3.4 %all-to-all-start.1 = ((bf16[8,128,128]{2,1,0:T(8,128)(2,1)}), bf16[8,128,128]{2,1,0:T(8,128)(2,1)S(1)}, u32[]{:S(2)}, u32[]{:S(2)}) async-start(bf16[8,128,128]{2,1,0:T(8,128)(2,1)} %collect.1), calls=%async_computation.1 | async-start | bytes 524288 | tf_op jit(solution)/shard_map/all_to_all | solution.py:214
  54.5 3.2 %spread_back.1 = (f32[8,128,128]{2,1,0:T(8,128)S(1)}, bf16[8,128,128]{2,1,0:T(8,128)(2,1)S(1)}) custom-call(s32[1]{0:T(128)} %bitcast.3.core, s32[128]{0:T(128)} %bitcast.16, s32[128]{0:T(128)} %bitcast.19, bf16[128,128,128]{2,1,0:T(8,128)(2,1)} %bitcast.13, bf16[16,256,128]{2,1,0:T(8,128)(2,1)S(1)} %all_to_all.25.received), custom_call_target="tpu_custom_call" | custom-call | flops 536870912 | bytes 6291456 | tf_op jit(solution)/shard_map/spread_back/pallas_call | solution.py:259
  57.6 1.8 %collective-permute-start = (bf16[8,128,128]{2,1,0:T(8,128)(2,1)S(1)}, bf16[8,128,128]{2,1,0:T(8,128)(2,1)S(1)}, u32[]{:S(2)}, u32[]{:S(2)}) collective-permute-start(bf16[8,128,128]{2,1,0:T(8,128)(2,1)S(1)} %get-tuple-element.21), channel_id=1, source_target_pairs={{0,16},{16,0},{32,48},{48,32},{64,80},{80,64},{96,112},{112,96},{1... | collective-permute-start | bytes 786440 | tf_op jit(solution)/shard_map/ppermute | solution.py:226
  59.5 1.2 %collective-permute-done.got = bf16[8,128,128]{2,1,0:T(8,128)(2,1)S(1)} collective-permute-done((bf16[8,128,128]{2,1,0:T(8,128)(2,1)S(1)}, bf16[8,128,128]{2,1,0:T(8,128)(2,1)S(1)}, u32[]{:S(2)}, u32[]{:S(2)}) %collective-permute-start) | collective-permute-done | bytes 262176 | tf_op jit(solution)/shard_map/ppermute | solution.py:226
  60.7 0.8 all-to-all-done.1
  61.5 0.0 copy-done
  61.5 3.2 %dense.1 = (bf16[8,128,128]{2,1,0:T(8,128)(2,1)S(1)}, f32[16,32,128]{2,1,0:T(8,128)S(1)}, f32[16,32,128]{2,1,0:T(8,128)S(1)}) custom-call(s32[1]{0:T(128)} %bitcast.3.core, bf16[4,256,128]{2,1,0:T(8,128)(2,1)S(1)} %bitcast.11, f32[8,128,128]{2,1,0:T(8,128)S(1)} %get-tuple-element.20.keep, bf16[8,128,128]{2,1,0:T(8,128)(2,1)S(1)} %collective-permute-done.got, ...), custom_call_target="tpu_custom_call" | custom-call | flops 1342177280 | bytes 6291456 | tf_op jit(solution)/shard_map/dense/pallas_call | solution.py:265
  64.7 3.3 %collective-permute-start.1 = (f32[16,32,128]{2,1,0:T(8,128)S(1)}, f32[16,32,128]{2,1,0:T(8,128)S(1)}, u32[]{:S(2)}, u32[]{:S(2)}) collective-permute-start(f32[16,32,128]{2,1,0:T(8,128)S(1)} %get-tuple-element.24), channel_id=1, source_target_pairs={{0,16},{16,0},{32,48},{48,32},{64,80},{80,64},{96,112},{112,96},{1... | collective-permute-start | bytes 786440 | tf_op jit(solution)/shard_map/ppermute | solution.py:226
  68.0 1.2 %collective-permute-done.1.got = f32[16,32,128]{2,1,0:T(8,128)S(1)} collective-permute-done((f32[16,32,128]{2,1,0:T(8,128)S(1)}, f32[16,32,128]{2,1,0:T(8,128)S(1)}, u32[]{:S(2)}, u32[]{:S(2)}) %collective-permute-start.1) | collective-permute-done | bytes 262176 | tf_op jit(solution)/shard_map/ppermute | solution.py:226
  69.2 11.0 %all_to_all.26.terms = bf16[16,64,128]{2,1,0:T(8,128)(2,1)S(1)} all-to-all(bf16[16,64,128]{2,1,0:T(8,128)(2,1)S(1)} %merge.1), channel_id=1, replica_groups=mesh['row'=16,'col'=16] {'col'}, dimensions={0} | all-to-all | bytes 524288 | tf_op jit(solution)/shard_map/all_to_all | solution.py:214
  80.2 0.7 share.1
  80.9 4.2 %all-to-all-start.3 = ((f32[8,32,128]{2,1,0:T(8,128)}), f32[8,32,128]{2,1,0:T(8,128)S(1)}, u32[]{:S(2)}, u32[]{:S(2)}) async-start(f32[8,32,128]{2,1,0:T(8,128)} %share.1), calls=%async_computation.3 | async-start | bytes 262144 | tf_op jit(solution)/shard_map/all_to_all | solution.py:214
  85.1 3.6 %all-gather.1 = bf16[16,128,128]{2,1,0:T(8,128)(2,1)S(1)} all-gather(bf16[8,128,128]{2,1,0:T(8,128)(2,1)S(1)} %get-tuple-element.22), channel_id=3, replica_groups={{0,16},{32,48},{64,80},{96,112},{128,144},{160,176},{192,208},{224,240}..., dimensions={0}, use_global_device_ids=true | all-gather | bytes 786432 | tf_op jit(solution)/shard_map/all_gather | solution.py:222
  88.7 3.3 %spread_second.1 = bf16[16,160,128]{2,1,0:T(8,128)(2,1)S(1)} custom-call(s32[128]{0:T(128)} %bitcast.17, s32[128]{0:T(128)} %bitcast.20, bf16[128,128,128]{2,1,0:T(8,128)(2,1)} %bitcast.14, bf16[2,8,128,128]{3,2,1,0:T(8,128)(2,1)S(1)} %bitcast.8), custom_call_target="tpu_custom_call" | custom-call | flops 536870912 | bytes 6291456 | tf_op jit(solution)/shard_map/spread_second/pallas_call | solution.py:277
  92.0 0.0 all-to-all-done.3
  92.1 12.8 %all_to_all.27.second = bf16[16,160,128]{2,1,0:T(8,128)(2,1)S(1)} all-to-all(bf16[16,160,128]{2,1,0:T(8,128)(2,1)S(1)} %broadcast_dynamic-update-slice_fusion), channel_id=1, replica_groups=mesh['row'=16,'col'=16] {'col'}, dimensions={0} | all-to-all | bytes 1310720 | tf_op jit(solution)/shard_map/all_to_all | solution.py:214
  104.9 5.4 %all-gather.2 = bf16[32,32,128]{2,1,0:T(8,128)(2,1)S(1)} all-gather(bf16[16,32,128]{2,1,0:T(8,128)(2,1)S(1)} %slice.26), channel_id=4, replica_groups={{0,16},{32,48},{64,80},{96,112},{128,144},{160,176},{192,208},{224,240}..., dimensions={0}, use_global_device_ids=true | all-gather | bytes 393216 | tf_op jit(solution)/shard_map/all_gather | solution.py:222
  110.2 0.8 finish.1
  (5 shorter events, 0.1 us)
Async XLA Ops:
  27.0 34.5 %copy-start = (bf16[128,512]{1,0:T(8,128)(2,1)S(1)}, bf16[128,512]{1,0:T(8,128)(2,1)}, u32[]{:S(2)}) copy-start(bf16[128,512]{1,0:T(8,128)(2,1)} %w_in.1) | copy-start | bytes 393220
  27.0 34.5 %copy-start.1 = (bf16[512,128]{1,0:T(8,128)(2,1)S(1)}, bf16[512,128]{1,0:T(8,128)(2,1)}, u32[]{:S(2)}) copy-start(bf16[512,128]{1,0:T(8,128)(2,1)} %w_out.1) | copy-start | bytes 393220
  51.0 10.5 %all-to-all-start.1 = ((bf16[8,128,128]{2,1,0:T(8,128)(2,1)}), bf16[8,128,128]{2,1,0:T(8,128)(2,1)S(1)}, u32[]{:S(2)}, u32[]{:S(2)}) async-start(bf16[8,128,128]{2,1,0:T(8,128)(2,1)} %collect.1), calls=%async_computation.1 | async-start | bytes 524288 | tf_op jit(solution)/shard_map/all_to_all | solution.py:214
  57.6 3.0 %collective-permute-start = (bf16[8,128,128]{2,1,0:T(8,128)(2,1)S(1)}, bf16[8,128,128]{2,1,0:T(8,128)(2,1)S(1)}, u32[]{:S(2)}, u32[]{:S(2)}) collective-permute-start(bf16[8,128,128]{2,1,0:T(8,128)(2,1)S(1)} %get-tuple-element.21), channel_id=1, source_target_pairs={{0,16},{16,0},{32,48},{48,32},{64,80},{80,64},{96,112},{112,96},{1... | collective-permute-start | bytes 786440 | tf_op jit(solution)/shard_map/ppermute | solution.py:226
  64.7 4.5 %collective-permute-start.1 = (f32[16,32,128]{2,1,0:T(8,128)S(1)}, f32[16,32,128]{2,1,0:T(8,128)S(1)}, u32[]{:S(2)}, u32[]{:S(2)}) collective-permute-start(f32[16,32,128]{2,1,0:T(8,128)S(1)} %get-tuple-element.24), channel_id=1, source_target_pairs={{0,16},{16,0},{32,48},{48,32},{64,80},{80,64},{96,112},{112,96},{1... | collective-permute-start | bytes 786440 | tf_op jit(solution)/shard_map/ppermute | solution.py:226
  80.9 11.1 %all-to-all-start.3 = ((f32[8,32,128]{2,1,0:T(8,128)}), f32[8,32,128]{2,1,0:T(8,128)S(1)}, u32[]{:S(2)}, u32[]{:S(2)}) async-start(f32[8,32,128]{2,1,0:T(8,128)} %share.1), calls=%async_computation.3 | async-start | bytes 262144 | tf_op jit(solution)/shard_map/all_to_all | solution.py:214
